TPU v7x, 512 devices: a whole 4x8x8 slice. The times are simulated.
512 devices in a mesh: cuts: 16 (over x_lo, z), space: 32 (over y, x_hi, core).
Axes of the slice: x: 4 (x_hi: 2, x_lo: 2; x = x_hi * 2 + x_lo), y: 8, z: 8, core: 2. Of those that a mesh axis runs over, the one named last changes fastest.
Arguments:
- old_starts: float32 [16, 5, 64, 16, 256], P('cuts', None, 'space'), may hold values from -6 to 6
- initial: float32 [5, 64, 16, 256], P(None, 'space'), may hold values from -6 to 6
- blade_force: float32 [5, 64, 16, 256], P(None, 'space'), may hold values from -6 to 6
- blade_owner: int32 [16, 3], replicated, may hold values from 0 to 31, as said below
Outputs:
- new_ends: float32 [16, 5, 64, 16, 256], P('cuts', None, 'space')
- jumps: float32 [16, 5, 64, 16, 256], P('cuts', None, 'space')
Inputs may be any that keep to these rules, and one draw needn't show every extreme that they name: `blade_owner`: both the smallest and the largest block index occur in every draw.
All inputs are finite; a program needn't handle non-finite values.
Results may differ from a plain program's by a relative error of at most 0.0001.
Values sent between devices are 32-bit elements; how exact they have to be, the bound alone decides.
A program may use at most 64 MiB of HBM per device.

v0:
```python
import jax
import jax.numpy as jnp
from jax import lax
from jax.sharding import PartitionSpec as P

STEPS = 3


mach = 0.3
courant = 0.2
coarse_courant = 0.3


def with_halo(block, sides, width):
    for axis, dim in sides:
        count = lax.axis_size(axis)
        forward = [(i, i + 1) for i in range(count - 1)]
        backward = [(target, source) for source, target in forward]
        low = lax.ppermute(
            lax.slice_in_dim(block, block.shape[dim] - width, None, axis=dim), axis, forward
        )
        high = lax.ppermute(lax.slice_in_dim(block, 0, width, axis=dim), axis, backward)
        block = jnp.concatenate([low, block, high], axis=dim)
    return block


def from_behind(block, axis, distance):
    devices = range(lax.axis_size(axis))
    route = [(i - distance, i) for i in devices if i - distance in devices]
    return lax.ppermute(block, axis, route)


def flux_rate(padded, ratio):
    center = padded[:, 1:-1]
    x_diff = padded[:, 2:] - padded[:, :-2]
    x_second = padded[:, 2:] - 2.0 * center + padded[:, :-2]
    y_upper = jnp.roll(center, -1, axis=2)
    y_lower = jnp.roll(center, 1, axis=2)
    z_upper = jnp.roll(center, -1, axis=3)
    z_lower = jnp.roll(center, 1, axis=3)
    y_diff = y_upper - y_lower
    z_diff = z_upper - z_lower
    y_second = y_upper - 2.0 * center + y_lower
    z_second = z_upper - 2.0 * center + z_lower
    divergence = x_diff[1] + y_diff[2] + z_diff[3]
    coupling = jnp.stack([divergence, x_diff[4], y_diff[4], z_diff[4], divergence])
    return -0.5 * ratio * (mach * x_diff + coupling) + 0.5 * ratio * (
        (mach + 1.0) * x_second + y_second + z_second
    )


def restrict(field):
    shape = field.shape
    blocks = field.reshape(shape[0], shape[1] // 2, 2, shape[2] // 2, 2, shape[3] // 2, 2)
    return jnp.mean(blocks, axis=(2, 4, 6))


def prolong(field):
    return jnp.repeat(jnp.repeat(jnp.repeat(field, 2, axis=1), 2, axis=2), 2, axis=3)


def fine_rate(state):
    padded = with_halo(state, (("space", 1),), 1)
    return flux_rate(padded, courant)


def coarse_step(coarse, source):
    padded = with_halo(coarse, (("space", 1),), 1)
    return coarse + flux_rate(padded, coarse_courant) + source


def body(old_starts, initial, blade_force, blade_owner):
    block = lax.axis_index("space")
    slice_index = lax.axis_index("cuts")
    owners = lax.dynamic_index_in_dim(blade_owner, slice_index, 0, keepdims=False)
    hits = (owners == block).astype(jnp.float32)
    start_old = old_starts[0]
    state = start_old
    for step in range(STEPS):
        source = courant * hits[step] * blade_force
        first = state + fine_rate(state) + source
        state = 0.5 * (state + first + fine_rate(first) + source)
    restricted_force = restrict(blade_force)
    step_count = jnp.sum(hits)
    coarse_source = courant * step_count * restricted_force
    coarse_old = coarse_step(restrict(start_old), coarse_source)
    correction = state - prolong(coarse_old)
    received = from_behind(state, "cuts", 1)
    first_slice = slice_index == 0
    jump = start_old - jnp.where(first_slice, initial, received)
    turns = lax.axis_size("cuts")

    def advance_fine(turn, end_state):
        arrived = from_behind(end_state, "cuts", 1)
        begin = jnp.where(first_slice, initial, arrived)
        return prolong(coarse_step(restrict(begin), coarse_source)) + correction

    new_end = lax.fori_loop(0, turns, advance_fine, jnp.zeros_like(initial))
    return (new_end[None], jump[None])


def solution(mesh):
    placed = (
        P("cuts", None, "space", None, None),
        P(None, "space", None, None),
        P(None, "space", None, None),
        P(),
    )
    return jax.shard_map(
        body,
        mesh=mesh,
        in_specs=placed,
        out_specs=(P("cuts", None, "space", None, None), P("cuts", None, "space", None, None)),
        check_vma=False,
    )
```

profile of v0, /device:TPU:31, one launch (start us, length us, event | category | flops | bytes accessed | tf_op | source)
XLA Modules:
  0.0 491.6 jit_solution(761058335786293518)
XLA Ops:
  13.9 7.3 %collective-permute-start.4 = (f32[5,1,16,256]{3,2,1,0:T(8,128)S(1)}, f32[5,1,16,256]{3,2,1,0:T(8,128)S(1)}, u32[]{:S(2)}, u32[]{:S(2)}) collective-permute-start(f32[5,1,16,256]{3,2,1,0:T(8,128)S(1)} %get-tuple-element.185), channel_id=1, source_target_pairs={{0,1},{1,2},{2,3},{3,4},{4,5},{5,6},{6,7},{7,8},{8,9},{9,10},{10,1... | collective-permute-start | bytes 245768 | tf_op jit(solution)/shard_map/ppermute | solution.py:19
  29.0 7.3 %collective-permute-start.6 = (f32[5,1,16,256]{3,2,1,0:T(8,128)S(1)}, f32[5,1,16,256]{3,2,1,0:T(8,128)S(1)}, u32[]{:S(2)}, u32[]{:S(2)}) collective-permute-start(f32[5,1,16,256]{3,2,1,0:T(8,128)S(1)} %get-tuple-element.175), channel_id=1, source_target_pairs={{0,1},{1,2},{2,3},{3,4},{4,5},{5,6},{6,7},{7,8},{8,9},{9,10},{10,1... | collective-permute-start | bytes 245768 | tf_op jit(solution)/shard_map/ppermute | solution.py:19
  40.3 7.9 %collective-permute-start.8 = (f32[5,1,16,256]{3,2,1,0:T(8,128)S(1)}, f32[5,1,16,256]{3,2,1,0:T(8,128)S(1)}, u32[]{:S(2)}, u32[]{:S(2)}) collective-permute-start(f32[5,1,16,256]{3,2,1,0:T(8,128)S(1)} %get-tuple-element.165), channel_id=1, source_target_pairs={{0,1},{1,2},{2,3},{3,4},{4,5},{5,6},{6,7},{7,8},{8,9},{9,10},{10,1... | collective-permute-start | bytes 245768 | tf_op jit(solution)/shard_map/ppermute | solution.py:19
  52.2 7.9 %collective-permute-start.10 = (f32[5,1,16,256]{3,2,1,0:T(8,128)S(1)}, f32[5,1,16,256]{3,2,1,0:T(8,128)S(1)}, u32[]{:S(2)}, u32[]{:S(2)}) collective-permute-start(f32[5,1,16,256]{3,2,1,0:T(8,128)S(1)} %get-tuple-element.155), channel_id=1, source_target_pairs={{0,1},{1,2},{2,3},{3,4},{4,5},{5,6},{6,7},{7,8},{8,9},{9,10},{10,1... | collective-permute-start | bytes 245768 | tf_op jit(solution)/shard_map/ppermute | solution.py:19
  64.1 7.9 %collective-permute-start.12 = (f32[5,1,16,256]{3,2,1,0:T(8,128)S(1)}, f32[5,1,16,256]{3,2,1,0:T(8,128)S(1)}, u32[]{:S(2)}, u32[]{:S(2)}) collective-permute-start(f32[5,1,16,256]{3,2,1,0:T(8,128)S(1)} %get-tuple-element.145), channel_id=1, source_target_pairs={{0,1},{1,2},{2,3},{3,4},{4,5},{5,6},{6,7},{7,8},{8,9},{9,10},{10,1... | collective-permute-start | bytes 245768 | tf_op jit(solution)/shard_map/ppermute | solution.py:19
  85.0 7.9 %collective-permute-start.14 = (f32[5,1,16,256]{3,2,1,0:T(8,128)S(1)}, f32[5,1,16,256]{3,2,1,0:T(8,128)S(1)}, u32[]{:S(2)}, u32[]{:S(2)}) collective-permute-start(f32[5,1,16,256]{3,2,1,0:T(8,128)S(1)} %copy-done.19), channel_id=1, source_target_pairs={{0,1},{1,2},{2,3},{3,4},{4,5},{5,6},{6,7},{7,8},{8,9},{9,10},{10,1... | collective-permute-start | bytes 245768 | tf_op jit(solution)/shard_map/ppermute | solution.py:19
  99.0 8.5 %collective-permute-done.17 = f32[5,2,16,256]{3,2,1,0:T(8,128)S(1)} collective-permute-done((f32[5,2,16,256]{3,2,1,0:T(8,128)S(1)}, f32[5,2,16,256]{3,2,1,0:T(8,128)S(1)}, u32[]{:S(2)}, u32[]{:S(2)}) %collective-permute-start.17) | collective-permute-done | bytes 163872 | tf_op jit(solution)/shard_map/ppermute | solution.py:30
  108.2 382.7 %while.13 = (s32[]{:T(128)}, f32[5,2,16,256]{3,2,1,0:T(8,128)S(1)}, pred[]{:T(512)}, f32[5,2,16,256]{3,2,1,0:T(8,128)S(1)}, f32[5,1,8,128]{3,2,1,0:T(8,128)S(1)}...) while((s32[]{:T(128)}, f32[5,2,16,256]{3,2,1,0:T(8,128)S(1)}, ...), condition=%wide.region_8.9_spmd.clone, body=%wide.region_5.8_spmd.clone.sunk | while | flops 316418 | bytes 3375332 | solution.py:98
  110.2 6.3 %collective-permute-done = f32[5,2,16,256]{3,2,1,0:T(8,128)S(1)} collective-permute-done((f32[5,2,16,256]{3,2,1,0:T(8,128)S(1)}, f32[5,2,16,256]{3,2,1,0:T(8,128)S(1)}, u32[]{:S(2)}, u32[]{:S(2)}) %collective-permute-start) | collective-permute-done | bytes 163872 | tf_op jit(solution)/shard_map/while/body/eval_jaxpr/ppermute | solution.py:30
  119.1 10.7 %collective-permute-start.1 = (f32[5,1,8,128]{3,2,1,0:T(8,128)S(1)}, f32[5,1,8,128]{3,2,1,0:T(8,128)S(1)}, u32[]{:S(2)}, u32[]{:S(2)}) collective-permute-start(f32[5,1,8,128]{3,2,1,0:T(8,128)S(1)} %multiply_bitcast_fusion.5), channel_id=1, source_target_pairs={{0,1},{1,2},{2,3},{3,4},{4,5},{5,6},{6,7},{7,8},{8,9},{9,10},{10,1... | collective-permute-start | bytes 61448 | tf_op jit(solution)/shard_map/while/body/eval_jaxpr/ppermute | solution.py:19
  132.0 6.5 %collective-permute-done.2 = f32[5,1,8,128]{3,2,1,0:T(8,128)S(1)} collective-permute-done((f32[5,1,8,128]{3,2,1,0:T(8,128)S(1)}, f32[5,1,8,128]{3,2,1,0:T(8,128)S(1)}, u32[]{:S(2)}, u32[]{:S(2)}) %collective-permute-start.2) | collective-permute-done | bytes 20512 | tf_op jit(solution)/shard_map/while/body/eval_jaxpr/ppermute | solution.py:22
  155.4 6.5 %collective-permute-done.2 = f32[5,1,8,128]{3,2,1,0:T(8,128)S(1)} collective-permute-done((f32[5,1,8,128]{3,2,1,0:T(8,128)S(1)}, f32[5,1,8,128]{3,2,1,0:T(8,128)S(1)}, u32[]{:S(2)}, u32[]{:S(2)}) %collective-permute-start.2) | collective-permute-done | bytes 20512 | tf_op jit(solution)/shard_map/while/body/eval_jaxpr/ppermute | solution.py:22
  164.7 6.2 %collective-permute-done = f32[5,2,16,256]{3,2,1,0:T(8,128)S(1)} collective-permute-done((f32[5,2,16,256]{3,2,1,0:T(8,128)S(1)}, f32[5,2,16,256]{3,2,1,0:T(8,128)S(1)}, u32[]{:S(2)}, u32[]{:S(2)}) %collective-permute-start) | collective-permute-done | bytes 163872 | tf_op jit(solution)/shard_map/while/body/eval_jaxpr/ppermute | solution.py:30
  178.8 6.5 %collective-permute-done.2 = f32[5,1,8,128]{3,2,1,0:T(8,128)S(1)} collective-permute-done((f32[5,1,8,128]{3,2,1,0:T(8,128)S(1)}, f32[5,1,8,128]{3,2,1,0:T(8,128)S(1)}, u32[]{:S(2)}, u32[]{:S(2)}) %collective-permute-start.2) | collective-permute-done | bytes 20512 | tf_op jit(solution)/shard_map/while/body/eval_jaxpr/ppermute | solution.py:22
  188.1 6.2 %collective-permute-done = f32[5,2,16,256]{3,2,1,0:T(8,128)S(1)} collective-permute-done((f32[5,2,16,256]{3,2,1,0:T(8,128)S(1)}, f32[5,2,16,256]{3,2,1,0:T(8,128)S(1)}, u32[]{:S(2)}, u32[]{:S(2)}) %collective-permute-start) | collective-permute-done | bytes 163872 | tf_op jit(solution)/shard_map/while/body/eval_jaxpr/ppermute | solution.py:30
  202.2 6.5 %collective-permute-done.2 = f32[5,1,8,128]{3,2,1,0:T(8,128)S(1)} collective-permute-done((f32[5,1,8,128]{3,2,1,0:T(8,128)S(1)}, f32[5,1,8,128]{3,2,1,0:T(8,128)S(1)}, u32[]{:S(2)}, u32[]{:S(2)}) %collective-permute-start.2) | collective-permute-done | bytes 20512 | tf_op jit(solution)/shard_map/while/body/eval_jaxpr/ppermute | solution.py:22
  211.5 6.2 %collective-permute-done = f32[5,2,16,256]{3,2,1,0:T(8,128)S(1)} collective-permute-done((f32[5,2,16,256]{3,2,1,0:T(8,128)S(1)}, f32[5,2,16,256]{3,2,1,0:T(8,128)S(1)}, u32[]{:S(2)}, u32[]{:S(2)}) %collective-permute-start) | collective-permute-done | bytes 163872 | tf_op jit(solution)/shard_map/while/body/eval_jaxpr/ppermute | solution.py:30
  225.6 6.5 %collective-permute-done.2 = f32[5,1,8,128]{3,2,1,0:T(8,128)S(1)} collective-permute-done((f32[5,1,8,128]{3,2,1,0:T(8,128)S(1)}, f32[5,1,8,128]{3,2,1,0:T(8,128)S(1)}, u32[]{:S(2)}, u32[]{:S(2)}) %collective-permute-start.2) | collective-permute-done | bytes 20512 | tf_op jit(solution)/shard_map/while/body/eval_jaxpr/ppermute | solution.py:22
  234.9 6.2 %collective-permute-done = f32[5,2,16,256]{3,2,1,0:T(8,128)S(1)} collective-permute-done((f32[5,2,16,256]{3,2,1,0:T(8,128)S(1)}, f32[5,2,16,256]{3,2,1,0:T(8,128)S(1)}, u32[]{:S(2)}, u32[]{:S(2)}) %collective-permute-start) | collective-permute-done | bytes 163872 | tf_op jit(solution)/shard_map/while/body/eval_jaxpr/ppermute | solution.py:30
  249.0 6.5 %collective-permute-done.2 = f32[5,1,8,128]{3,2,1,0:T(8,128)S(1)} collective-permute-done((f32[5,1,8,128]{3,2,1,0:T(8,128)S(1)}, f32[5,1,8,128]{3,2,1,0:T(8,128)S(1)}, u32[]{:S(2)}, u32[]{:S(2)}) %collective-permute-start.2) | collective-permute-done | bytes 20512 | tf_op jit(solution)/shard_map/while/body/eval_jaxpr/ppermute | solution.py:22
  272.5 6.5 %collective-permute-done.2 = f32[5,1,8,128]{3,2,1,0:T(8,128)S(1)} collective-permute-done((f32[5,1,8,128]{3,2,1,0:T(8,128)S(1)}, f32[5,1,8,128]{3,2,1,0:T(8,128)S(1)}, u32[]{:S(2)}, u32[]{:S(2)}) %collective-permute-start.2) | collective-permute-done | bytes 20512 | tf_op jit(solution)/shard_map/while/body/eval_jaxpr/ppermute | solution.py:22
  295.9 6.5 %collective-permute-done.2 = f32[5,1,8,128]{3,2,1,0:T(8,128)S(1)} collective-permute-done((f32[5,1,8,128]{3,2,1,0:T(8,128)S(1)}, f32[5,1,8,128]{3,2,1,0:T(8,128)S(1)}, u32[]{:S(2)}, u32[]{:S(2)}) %collective-permute-start.2) | collective-permute-done | bytes 20512 | tf_op jit(solution)/shard_map/while/body/eval_jaxpr/ppermute | solution.py:22
  319.3 6.5 %collective-permute-done.2 = f32[5,1,8,128]{3,2,1,0:T(8,128)S(1)} collective-permute-done((f32[5,1,8,128]{3,2,1,0:T(8,128)S(1)}, f32[5,1,8,128]{3,2,1,0:T(8,128)S(1)}, u32[]{:S(2)}, u32[]{:S(2)}) %collective-permute-start.2) | collective-permute-done | bytes 20512 | tf_op jit(solution)/shard_map/while/body/eval_jaxpr/ppermute | solution.py:22
  342.7 6.5 %collective-permute-done.2 = f32[5,1,8,128]{3,2,1,0:T(8,128)S(1)} collective-permute-done((f32[5,1,8,128]{3,2,1,0:T(8,128)S(1)}, f32[5,1,8,128]{3,2,1,0:T(8,128)S(1)}, u32[]{:S(2)}, u32[]{:S(2)}) %collective-permute-start.2) | collective-permute-done | bytes 20512 | tf_op jit(solution)/shard_map/while/body/eval_jaxpr/ppermute | solution.py:22
  366.3 6.5 %collective-permute-done.2 = f32[5,1,8,128]{3,2,1,0:T(8,128)S(1)} collective-permute-done((f32[5,1,8,128]{3,2,1,0:T(8,128)S(1)}, f32[5,1,8,128]{3,2,1,0:T(8,128)S(1)}, u32[]{:S(2)}, u32[]{:S(2)}) %collective-permute-start.2) | collective-permute-done | bytes 20512 | tf_op jit(solution)/shard_map/while/body/eval_jaxpr/ppermute | solution.py:22
  389.7 6.5 %collective-permute-done.2 = f32[5,1,8,128]{3,2,1,0:T(8,128)S(1)} collective-permute-done((f32[5,1,8,128]{3,2,1,0:T(8,128)S(1)}, f32[5,1,8,128]{3,2,1,0:T(8,128)S(1)}, u32[]{:S(2)}, u32[]{:S(2)}) %collective-permute-start.2) | collective-permute-done | bytes 20512 | tf_op jit(solution)/shard_map/while/body/eval_jaxpr/ppermute | solution.py:22
  399.0 6.5 %collective-permute-done = f32[5,2,16,256]{3,2,1,0:T(8,128)S(1)} collective-permute-done((f32[5,2,16,256]{3,2,1,0:T(8,128)S(1)}, f32[5,2,16,256]{3,2,1,0:T(8,128)S(1)}, u32[]{:S(2)}, u32[]{:S(2)}) %collective-permute-start) | collective-permute-done | bytes 163872 | tf_op jit(solution)/shard_map/while/body/eval_jaxpr/ppermute | solution.py:30
  413.2 6.5 %collective-permute-done.2 = f32[5,1,8,128]{3,2,1,0:T(8,128)S(1)} collective-permute-done((f32[5,1,8,128]{3,2,1,0:T(8,128)S(1)}, f32[5,1,8,128]{3,2,1,0:T(8,128)S(1)}, u32[]{:S(2)}, u32[]{:S(2)}) %collective-permute-start.2) | collective-permute-done | bytes 20512 | tf_op jit(solution)/shard_map/while/body/eval_jaxpr/ppermute | solution.py:22
  422.5 6.5 %collective-permute-done = f32[5,2,16,256]{3,2,1,0:T(8,128)S(1)} collective-permute-done((f32[5,2,16,256]{3,2,1,0:T(8,128)S(1)}, f32[5,2,16,256]{3,2,1,0:T(8,128)S(1)}, u32[]{:S(2)}, u32[]{:S(2)}) %collective-permute-start) | collective-permute-done | bytes 163872 | tf_op jit(solution)/shard_map/while/body/eval_jaxpr/ppermute | solution.py:30
  436.6 6.5 %collective-permute-done.2 = f32[5,1,8,128]{3,2,1,0:T(8,128)S(1)} collective-permute-done((f32[5,1,8,128]{3,2,1,0:T(8,128)S(1)}, f32[5,1,8,128]{3,2,1,0:T(8,128)S(1)}, u32[]{:S(2)}, u32[]{:S(2)}) %collective-permute-start.2) | collective-permute-done | bytes 20512 | tf_op jit(solution)/shard_map/while/body/eval_jaxpr/ppermute | solution.py:22
  460.2 6.5 %collective-permute-done.2 = f32[5,1,8,128]{3,2,1,0:T(8,128)S(1)} collective-permute-done((f32[5,1,8,128]{3,2,1,0:T(8,128)S(1)}, f32[5,1,8,128]{3,2,1,0:T(8,128)S(1)}, u32[]{:S(2)}, u32[]{:S(2)}) %collective-permute-start.2) | collective-permute-done | bytes 20512 | tf_op jit(solution)/shard_map/while/body/eval_jaxpr/ppermute | solution.py:22
  483.6 6.5 %collective-permute-done.2 = f32[5,1,8,128]{3,2,1,0:T(8,128)S(1)} collective-permute-done((f32[5,1,8,128]{3,2,1,0:T(8,128)S(1)}, f32[5,1,8,128]{3,2,1,0:T(8,128)S(1)}, u32[]{:S(2)}, u32[]{:S(2)}) %collective-permute-start.2) | collective-permute-done | bytes 20512 | tf_op jit(solution)/shard_map/while/body/eval_jaxpr/ppermute | solution.py:22
  (624 shorter events, 271.1 us)
Async XLA Ops:
  4.2 21.6 %collective-permute-start.16 = (f32[5,1,8,128]{3,2,1,0:T(8,128)S(1)}, f32[5,1,8,128]{3,2,1,0:T(8,128)S(1)}, u32[]{:S(2)}, u32[]{:S(2)}) collective-permute-start(f32[5,1,8,128]{3,2,1,0:T(8,128)S(1)} %multiply_bitcast_fusion.1), channel_id=1, source_target_pairs={{0,1},{1,2},{2,3},{3,4},{4,5},{5,6},{6,7},{7,8},{8,9},{9,10},{10,1... | collective-permute-start | bytes 61448 | tf_op jit(solution)/shard_map/ppermute | solution.py:19
  10.0 15.8 %collective-permute-start.15 = (f32[5,1,8,128]{3,2,1,0:T(8,128)S(1)}, f32[5,1,8,128]{3,2,1,0:T(8,128)S(1)}, u32[]{:S(2)}, u32[]{:S(2)}) collective-permute-start(f32[5,1,8,128]{3,2,1,0:T(8,128)S(1)} %multiply_bitcast_fusion.1), channel_id=1, source_target_pairs={{1,0},{2,1},{3,2},{4,3},{5,4},{6,5},{7,6},{8,7},{9,8},{10,9},{11,1... | collective-permute-start | bytes 61448 | tf_op jit(solution)/shard_map/ppermute | solution.py:22
  12.0 13.9 %collective-permute-start.3 = (f32[5,1,16,256]{3,2,1,0:T(8,128)S(1)}, f32[5,1,16,256]{3,2,1,0:T(8,128)S(1)}, u32[]{:S(2)}, u32[]{:S(2)}) collective-permute-start(f32[5,1,16,256]{3,2,1,0:T(8,128)S(1)} %get-tuple-element.186), channel_id=1, source_target_pairs={{1,0},{2,1},{3,2},{4,3},{5,4},{6,5},{7,6},{8,7},{9,8},{10,9},{11,1... | collective-permute-start | bytes 245768 | tf_op jit(solution)/shard_map/ppermute | solution.py:22
  13.9 12.5 %collective-permute-start.4 = (f32[5,1,16,256]{3,2,1,0:T(8,128)S(1)}, f32[5,1,16,256]{3,2,1,0:T(8,128)S(1)}, u32[]{:S(2)}, u32[]{:S(2)}) collective-permute-start(f32[5,1,16,256]{3,2,1,0:T(8,128)S(1)} %get-tuple-element.185), channel_id=1, source_target_pairs={{0,1},{1,2},{2,3},{3,4},{4,5},{5,6},{6,7},{7,8},{8,9},{9,10},{10,1... | collective-permute-start | bytes 245768 | tf_op jit(solution)/shard_map/ppermute | solution.py:19
  27.1 9.4 %collective-permute-start.5 = (f32[5,1,16,256]{3,2,1,0:T(8,128)S(1)}, f32[5,1,16,256]{3,2,1,0:T(8,128)S(1)}, u32[]{:S(2)}, u32[]{:S(2)}) collective-permute-start(f32[5,1,16,256]{3,2,1,0:T(8,128)S(1)} %get-tuple-element.176), channel_id=1, source_target_pairs={{1,0},{2,1},{3,2},{4,3},{5,4},{6,5},{7,6},{8,7},{9,8},{10,9},{11,1... | collective-permute-start | bytes 245768 | tf_op jit(solution)/shard_map/ppermute | solution.py:22
  29.0 8.7 %collective-permute-start.6 = (f32[5,1,16,256]{3,2,1,0:T(8,128)S(1)}, f32[5,1,16,256]{3,2,1,0:T(8,128)S(1)}, u32[]{:S(2)}, u32[]{:S(2)}) collective-permute-start(f32[5,1,16,256]{3,2,1,0:T(8,128)S(1)} %get-tuple-element.175), channel_id=1, source_target_pairs={{0,1},{1,2},{2,3},{3,4},{4,5},{5,6},{6,7},{7,8},{8,9},{9,10},{10,1... | collective-permute-start | bytes 245768 | tf_op jit(solution)/shard_map/ppermute | solution.py:19
  38.3 10.0 %collective-permute-start.7 = (f32[5,1,16,256]{3,2,1,0:T(8,128)S(1)}, f32[5,1,16,256]{3,2,1,0:T(8,128)S(1)}, u32[]{:S(2)}, u32[]{:S(2)}) collective-permute-start(f32[5,1,16,256]{3,2,1,0:T(8,128)S(1)} %get-tuple-element.166), channel_id=1, source_target_pairs={{1,0},{2,1},{3,2},{4,3},{5,4},{6,5},{7,6},{8,7},{9,8},{10,9},{11,1... | collective-permute-start | bytes 245768 | tf_op jit(solution)/shard_map/ppermute | solution.py:22
  40.3 9.4 %collective-permute-start.8 = (f32[5,1,16,256]{3,2,1,0:T(8,128)S(1)}, f32[5,1,16,256]{3,2,1,0:T(8,128)S(1)}, u32[]{:S(2)}, u32[]{:S(2)}) collective-permute-start(f32[5,1,16,256]{3,2,1,0:T(8,128)S(1)} %get-tuple-element.165), channel_id=1, source_target_pairs={{0,1},{1,2},{2,3},{3,4},{4,5},{5,6},{6,7},{7,8},{8,9},{9,10},{10,1... | collective-permute-start | bytes 245768 | tf_op jit(solution)/shard_map/ppermute | solution.py:19
  50.3 10.0 %collective-permute-start.9 = (f32[5,1,16,256]{3,2,1,0:T(8,128)S(1)}, f32[5,1,16,256]{3,2,1,0:T(8,128)S(1)}, u32[]{:S(2)}, u32[]{:S(2)}) collective-permute-start(f32[5,1,16,256]{3,2,1,0:T(8,128)S(1)} %get-tuple-element.156), channel_id=1, source_target_pairs={{1,0},{2,1},{3,2},{4,3},{5,4},{6,5},{7,6},{8,7},{9,8},{10,9},{11,1... | collective-permute-start | bytes 245768 | tf_op jit(solution)/shard_map/ppermute | solution.py:22
  52.2 9.4 %collective-permute-start.10 = (f32[5,1,16,256]{3,2,1,0:T(8,128)S(1)}, f32[5,1,16,256]{3,2,1,0:T(8,128)S(1)}, u32[]{:S(2)}, u32[]{:S(2)}) collective-permute-start(f32[5,1,16,256]{3,2,1,0:T(8,128)S(1)} %get-tuple-element.155), channel_id=1, source_target_pairs={{0,1},{1,2},{2,3},{3,4},{4,5},{5,6},{6,7},{7,8},{8,9},{9,10},{10,1... | collective-permute-start | bytes 245768 | tf_op jit(solution)/shard_map/ppermute | solution.py:19
  62.2 10.0 %collective-permute-start.11 = (f32[5,1,16,256]{3,2,1,0:T(8,128)S(1)}, f32[5,1,16,256]{3,2,1,0:T(8,128)S(1)}, u32[]{:S(2)}, u32[]{:S(2)}) collective-permute-start(f32[5,1,16,256]{3,2,1,0:T(8,128)S(1)} %get-tuple-element.146), channel_id=1, source_target_pairs={{1,0},{2,1},{3,2},{4,3},{5,4},{6,5},{7,6},{8,7},{9,8},{10,9},{11,1... | collective-permute-start | bytes 245768 | tf_op jit(solution)/shard_map/ppermute | solution.py:22
  64.1 9.4 %collective-permute-start.12 = (f32[5,1,16,256]{3,2,1,0:T(8,128)S(1)}, f32[5,1,16,256]{3,2,1,0:T(8,128)S(1)}, u32[]{:S(2)}, u32[]{:S(2)}) collective-permute-start(f32[5,1,16,256]{3,2,1,0:T(8,128)S(1)} %get-tuple-element.145), channel_id=1, source_target_pairs={{0,1},{1,2},{2,3},{3,4},{4,5},{5,6},{6,7},{7,8},{8,9},{9,10},{10,1... | collective-permute-start | bytes 245768 | tf_op jit(solution)/shard_map/ppermute | solution.py:19
  83.1 10.1 %collective-permute-start.13 = (f32[5,1,16,256]{3,2,1,0:T(8,128)S(1)}, f32[5,1,16,256]{3,2,1,0:T(8,128)S(1)}, u32[]{:S(2)}, u32[]{:S(2)}) collective-permute-start(f32[5,1,16,256]{3,2,1,0:T(8,128)S(1)} %copy-done.20), channel_id=1, source_target_pairs={{1,0},{2,1},{3,2},{4,3},{5,4},{6,5},{7,6},{8,7},{9,8},{10,9},{11,1... | collective-permute-start | bytes 245768 | tf_op jit(solution)/shard_map/ppermute | solution.py:22
  85.0 9.4 %collective-permute-start.14 = (f32[5,1,16,256]{3,2,1,0:T(8,128)S(1)}, f32[5,1,16,256]{3,2,1,0:T(8,128)S(1)}, u32[]{:S(2)}, u32[]{:S(2)}) collective-permute-start(f32[5,1,16,256]{3,2,1,0:T(8,128)S(1)} %copy-done.19), channel_id=1, source_target_pairs={{0,1},{1,2},{2,3},{3,4},{4,5},{5,6},{6,7},{7,8},{8,9},{9,10},{10,1... | collective-permute-start | bytes 245768 | tf_op jit(solution)/shard_map/ppermute | solution.py:19
  94.8 12.7 %collective-permute-start.17 = (f32[5,2,16,256]{3,2,1,0:T(8,128)S(1)}, f32[5,2,16,256]{3,2,1,0:T(8,128)S(1)}, u32[]{:S(2)}, u32[]{:S(2)}) collective-permute-start(f32[5,2,16,256]{3,2,1,0:T(8,128)S(1)} %get-tuple-element.114), channel_id=1, source_target_pairs={{0,32},{32,64},{64,96},{96,128},{128,160},{160,192},{192,224},{224... | collective-permute-start | bytes 491528 | tf_op jit(solution)/shard_map/ppermute | solution.py:30
  119.1 12.9 %collective-permute-start.1 = (f32[5,1,8,128]{3,2,1,0:T(8,128)S(1)}, f32[5,1,8,128]{3,2,1,0:T(8,128)S(1)}, u32[]{:S(2)}, u32[]{:S(2)}) collective-permute-start(f32[5,1,8,128]{3,2,1,0:T(8,128)S(1)} %multiply_bitcast_fusion.5), channel_id=1, source_target_pairs={{0,1},{1,2},{2,3},{3,4},{4,5},{5,6},{6,7},{7,8},{8,9},{9,10},{10,1... | collective-permute-start | bytes 61448 | tf_op jit(solution)/shard_map/while/body/eval_jaxpr/ppermute | solution.py:19
  129.8 8.7 %collective-permute-start.2 = (f32[5,1,8,128]{3,2,1,0:T(8,128)S(1)}, f32[5,1,8,128]{3,2,1,0:T(8,128)S(1)}, u32[]{:S(2)}, u32[]{:S(2)}) collective-permute-start(f32[5,1,8,128]{3,2,1,0:T(8,128)S(1)} %multiply_bitcast_fusion.5), channel_id=1, source_target_pairs={{1,0},{2,1},{3,2},{4,3},{5,4},{6,5},{7,6},{8,7},{9,8},{10,9},{11,1... | collective-permute-start | bytes 61448 | tf_op jit(solution)/shard_map/while/body/eval_jaxpr/ppermute | solution.py:22
  153.2 8.7 %collective-permute-start.2 = (f32[5,1,8,128]{3,2,1,0:T(8,128)S(1)}, f32[5,1,8,128]{3,2,1,0:T(8,128)S(1)}, u32[]{:S(2)}, u32[]{:S(2)}) collective-permute-start(f32[5,1,8,128]{3,2,1,0:T(8,128)S(1)} %multiply_bitcast_fusion.5), channel_id=1, source_target_pairs={{1,0},{2,1},{3,2},{4,3},{5,4},{6,5},{7,6},{8,7},{9,8},{10,9},{11,1... | collective-permute-start | bytes 61448 | tf_op jit(solution)/shard_map/while/body/eval_jaxpr/ppermute | solution.py:22
  176.6 8.7 %collective-permute-start.2 = (f32[5,1,8,128]{3,2,1,0:T(8,128)S(1)}, f32[5,1,8,128]{3,2,1,0:T(8,128)S(1)}, u32[]{:S(2)}, u32[]{:S(2)}) collective-permute-start(f32[5,1,8,128]{3,2,1,0:T(8,128)S(1)} %multiply_bitcast_fusion.5), channel_id=1, source_target_pairs={{1,0},{2,1},{3,2},{4,3},{5,4},{6,5},{7,6},{8,7},{9,8},{10,9},{11,1... | collective-permute-start | bytes 61448 | tf_op jit(solution)/shard_map/while/body/eval_jaxpr/ppermute | solution.py:22
  200.0 8.7 %collective-permute-start.2 = (f32[5,1,8,128]{3,2,1,0:T(8,128)S(1)}, f32[5,1,8,128]{3,2,1,0:T(8,128)S(1)}, u32[]{:S(2)}, u32[]{:S(2)}) collective-permute-start(f32[5,1,8,128]{3,2,1,0:T(8,128)S(1)} %multiply_bitcast_fusion.5), channel_id=1, source_target_pairs={{1,0},{2,1},{3,2},{4,3},{5,4},{6,5},{7,6},{8,7},{9,8},{10,9},{11,1... | collective-permute-start | bytes 61448 | tf_op jit(solution)/shard_map/while/body/eval_jaxpr/ppermute | solution.py:22
  223.4 8.7 %collective-permute-start.2 = (f32[5,1,8,128]{3,2,1,0:T(8,128)S(1)}, f32[5,1,8,128]{3,2,1,0:T(8,128)S(1)}, u32[]{:S(2)}, u32[]{:S(2)}) collective-permute-start(f32[5,1,8,128]{3,2,1,0:T(8,128)S(1)} %multiply_bitcast_fusion.5), channel_id=1, source_target_pairs={{1,0},{2,1},{3,2},{4,3},{5,4},{6,5},{7,6},{8,7},{9,8},{10,9},{11,1... | collective-permute-start | bytes 61448 | tf_op jit(solution)/shard_map/while/body/eval_jaxpr/ppermute | solution.py:22
  246.8 8.7 %collective-permute-start.2 = (f32[5,1,8,128]{3,2,1,0:T(8,128)S(1)}, f32[5,1,8,128]{3,2,1,0:T(8,128)S(1)}, u32[]{:S(2)}, u32[]{:S(2)}) collective-permute-start(f32[5,1,8,128]{3,2,1,0:T(8,128)S(1)} %multiply_bitcast_fusion.5), channel_id=1, source_target_pairs={{1,0},{2,1},{3,2},{4,3},{5,4},{6,5},{7,6},{8,7},{9,8},{10,9},{11,1... | collective-permute-start | bytes 61448 | tf_op jit(solution)/shard_map/while/body/eval_jaxpr/ppermute | solution.py:22
  270.2 8.7 %collective-permute-start.2 = (f32[5,1,8,128]{3,2,1,0:T(8,128)S(1)}, f32[5,1,8,128]{3,2,1,0:T(8,128)S(1)}, u32[]{:S(2)}, u32[]{:S(2)}) collective-permute-start(f32[5,1,8,128]{3,2,1,0:T(8,128)S(1)} %multiply_bitcast_fusion.5), channel_id=1, source_target_pairs={{1,0},{2,1},{3,2},{4,3},{5,4},{6,5},{7,6},{8,7},{9,8},{10,9},{11,1... | collective-permute-start | bytes 61448 | tf_op jit(solution)/shard_map/while/body/eval_jaxpr/ppermute | solution.py:22
  293.7 8.7 %collective-permute-start.2 = (f32[5,1,8,128]{3,2,1,0:T(8,128)S(1)}, f32[5,1,8,128]{3,2,1,0:T(8,128)S(1)}, u32[]{:S(2)}, u32[]{:S(2)}) collective-permute-start(f32[5,1,8,128]{3,2,1,0:T(8,128)S(1)} %multiply_bitcast_fusion.5), channel_id=1, source_target_pairs={{1,0},{2,1},{3,2},{4,3},{5,4},{6,5},{7,6},{8,7},{9,8},{10,9},{11,1... | collective-permute-start | bytes 61448 | tf_op jit(solution)/shard_map/while/body/eval_jaxpr/ppermute | solution.py:22
  317.1 8.7 %collective-permute-start.2 = (f32[5,1,8,128]{3,2,1,0:T(8,128)S(1)}, f32[5,1,8,128]{3,2,1,0:T(8,128)S(1)}, u32[]{:S(2)}, u32[]{:S(2)}) collective-permute-start(f32[5,1,8,128]{3,2,1,0:T(8,128)S(1)} %multiply_bitcast_fusion.5), channel_id=1, source_target_pairs={{1,0},{2,1},{3,2},{4,3},{5,4},{6,5},{7,6},{8,7},{9,8},{10,9},{11,1... | collective-permute-start | bytes 61448 | tf_op jit(solution)/shard_map/while/body/eval_jaxpr/ppermute | solution.py:22
  340.5 8.7 %collective-permute-start.2 = (f32[5,1,8,128]{3,2,1,0:T(8,128)S(1)}, f32[5,1,8,128]{3,2,1,0:T(8,128)S(1)}, u32[]{:S(2)}, u32[]{:S(2)}) collective-permute-start(f32[5,1,8,128]{3,2,1,0:T(8,128)S(1)} %multiply_bitcast_fusion.5), channel_id=1, source_target_pairs={{1,0},{2,1},{3,2},{4,3},{5,4},{6,5},{7,6},{8,7},{9,8},{10,9},{11,1... | collective-permute-start | bytes 61448 | tf_op jit(solution)/shard_map/while/body/eval_jaxpr/ppermute | solution.py:22
  364.1 8.7 %collective-permute-start.2 = (f32[5,1,8,128]{3,2,1,0:T(8,128)S(1)}, f32[5,1,8,128]{3,2,1,0:T(8,128)S(1)}, u32[]{:S(2)}, u32[]{:S(2)}) collective-permute-start(f32[5,1,8,128]{3,2,1,0:T(8,128)S(1)} %multiply_bitcast_fusion.5), channel_id=1, source_target_pairs={{1,0},{2,1},{3,2},{4,3},{5,4},{6,5},{7,6},{8,7},{9,8},{10,9},{11,1... | collective-permute-start | bytes 61448 | tf_op jit(solution)/shard_map/while/body/eval_jaxpr/ppermute | solution.py:22
  387.5 8.7 %collective-permute-start.2 = (f32[5,1,8,128]{3,2,1,0:T(8,128)S(1)}, f32[5,1,8,128]{3,2,1,0:T(8,128)S(1)}, u32[]{:S(2)}, u32[]{:S(2)}) collective-permute-start(f32[5,1,8,128]{3,2,1,0:T(8,128)S(1)} %multiply_bitcast_fusion.5), channel_id=1, source_target_pairs={{1,0},{2,1},{3,2},{4,3},{5,4},{6,5},{7,6},{8,7},{9,8},{10,9},{11,1... | collective-permute-start | bytes 61448 | tf_op jit(solution)/shard_map/while/body/eval_jaxpr/ppermute | solution.py:22
  411.0 8.7 %collective-permute-start.2 = (f32[5,1,8,128]{3,2,1,0:T(8,128)S(1)}, f32[5,1,8,128]{3,2,1,0:T(8,128)S(1)}, u32[]{:S(2)}, u32[]{:S(2)}) collective-permute-start(f32[5,1,8,128]{3,2,1,0:T(8,128)S(1)} %multiply_bitcast_fusion.5), channel_id=1, source_target_pairs={{1,0},{2,1},{3,2},{4,3},{5,4},{6,5},{7,6},{8,7},{9,8},{10,9},{11,1... | collective-permute-start | bytes 61448 | tf_op jit(solution)/shard_map/while/body/eval_jaxpr/ppermute | solution.py:22
  434.4 8.7 %collective-permute-start.2 = (f32[5,1,8,128]{3,2,1,0:T(8,128)S(1)}, f32[5,1,8,128]{3,2,1,0:T(8,128)S(1)}, u32[]{:S(2)}, u32[]{:S(2)}) collective-permute-start(f32[5,1,8,128]{3,2,1,0:T(8,128)S(1)} %multiply_bitcast_fusion.5), channel_id=1, source_target_pairs={{1,0},{2,1},{3,2},{4,3},{5,4},{6,5},{7,6},{8,7},{9,8},{10,9},{11,1... | collective-permute-start | bytes 61448 | tf_op jit(solution)/shard_map/while/body/eval_jaxpr/ppermute | solution.py:22
  458.0 8.7 %collective-permute-start.2 = (f32[5,1,8,128]{3,2,1,0:T(8,128)S(1)}, f32[5,1,8,128]{3,2,1,0:T(8,128)S(1)}, u32[]{:S(2)}, u32[]{:S(2)}) collective-permute-start(f32[5,1,8,128]{3,2,1,0:T(8,128)S(1)} %multiply_bitcast_fusion.5), channel_id=1, source_target_pairs={{1,0},{2,1},{3,2},{4,3},{5,4},{6,5},{7,6},{8,7},{9,8},{10,9},{11,1... | collective-permute-start | bytes 61448 | tf_op jit(solution)/shard_map/while/body/eval_jaxpr/ppermute | solution.py:22
  481.4 8.7 %collective-permute-start.2 = (f32[5,1,8,128]{3,2,1,0:T(8,128)S(1)}, f32[5,1,8,128]{3,2,1,0:T(8,128)S(1)}, u32[]{:S(2)}, u32[]{:S(2)}) collective-permute-start(f32[5,1,8,128]{3,2,1,0:T(8,128)S(1)} %multiply_bitcast_fusion.5), channel_id=1, source_target_pairs={{1,0},{2,1},{3,2},{4,3},{5,4},{6,5},{7,6},{8,7},{9,8},{10,9},{11,1... | collective-permute-start | bytes 61448 | tf_op jit(solution)/shard_map/while/body/eval_jaxpr/ppermute | solution.py:22
  (56 other events, 361.0 us)
where the time goes:
time: 494 us; the launch traced here: 492 us
  waiting for transfers between devices  219 us (44%)
  starting transfers between devices  188 us (38%)
  other arithmetic  41.9 us (8%)
  local copies, waits for them, and re-layouts  35.7 us (7%)
    ppermute x17, waiting for transfers between devices, from_behind(): return lax.ppermute(block, axis, route)  109 us
    ppermute x23, starting transfers between devices, with_halo(): lax.ppermute(lax.slice_in_dim(block, block.shape[dim] - width, None, axis...  109 us
    ppermute x23, waiting for transfers between devices, with_halo(): lax.ppermute(lax.slice_in_dim(block, 0, width, axis=dim), axis, backward)  104 us
    ppermute x23, starting transfers between devices, with_halo(): lax.ppermute(lax.slice_in_dim(block, 0, width, axis=dim), axis, backward)  44.2 us
    ppermute x17, starting transfers between devices, from_behind(): return lax.ppermute(block, axis, route)  34.9 us
    reduce_sum x35, other arithmetic, restrict(): return jnp.mean(blocks, axis=(2, 4, 6))  32.1 us
    reduce_sum x36, local copies, waits for them, and re-layouts, restrict(): return jnp.mean(blocks, axis=(2, 4, 6))  16 us
  transfers between devices with their start and end apart: 63, of which 38 were waited for; matrix products, arithmetic and copies ran while one was open for 1% of the time, Pallas kernels for 0%

commit v1 on v0

v1 whole, which is shorter than its diff:
```python
import functools

import jax
import jax.numpy as jnp
import numpy as np
from jax import lax
from jax.experimental import pallas as pl
from jax.experimental.pallas import tpu as pltpu
from jax.sharding import PartitionSpec as P

MESH = pl.DeviceIdType.MESH
HIGHEST = lax.Precision.HIGHEST

STEPS = 3
NVAR = 5
NY = 16
NZ = 256
SPACE = 32
CUTS = 16
LANES = 128
ROWS = 2 * NVAR * NY

mach = 0.3
courant = 0.2
coarse_courant = 0.3


def wave(count, k, phase):
    angle = 2.0 * np.pi * k * np.arange(count) / count
    v = np.cos(angle) if phase == 0 else np.sin(angle)
    return v / np.sqrt(np.sum(v * v))


def group_waves(g):
    if g == 0:
        fine = [(0, 0), (64, 0), (128, 0), (64, 1)]
        coarse = [(0, 0), (64, 0)]
    else:
        fine = [(g, 0), (128 - g, 0), (g, 1), (128 - g, 1)]
        coarse = [(g, 0), (g, 1)]
    return fine, coarse


def make_tables():
    half = NZ // 2
    restrict_z = np.zeros((half, NZ))
    for j in range(half):
        restrict_z[j, 2 * j : 2 * j + 2] = 0.5
    forward = np.zeros((8, SPACE, NZ))
    back_coarse = np.zeros((4, SPACE, NZ))
    lanes = np.zeros((SPACE, 16, 8, NY))
    even = (np.arange(NY) % 2 == 0).astype(np.float64)
    for t in range(SPACE):
        for q in range(2):
            fine, coarse = group_waves(t + 32 * q)
            basis = [wave(NZ, *w) for w in fine]
            coarse_basis = [wave(half, *w) for w in coarse]
            for i in range(4):
                slot = q + 2 * i
                forward[slot, t] = basis[i]
                upper, lower = np.roll(basis[i], -1), np.roll(basis[i], 1)
                lanes[t, 0, slot] = basis[i] @ (upper + lower) - 2.0
                partner = basis[(i + 2) % 4]
                lanes[t, 1, slot] = basis[i] @ (np.roll(partner, -1) - np.roll(partner, 1))
            for i in range(2):
                slot = q + 4 * i
                back_coarse[q + 2 * i, t] = np.repeat(coarse_basis[i], 2)
                upper, lower = np.roll(coarse_basis[i], -1), np.roll(coarse_basis[i], 1)
                lanes[t, 2, slot] = coarse_basis[i] @ (upper + lower) - 2.0
                partner = coarse_basis[1 - i]
                lanes[t, 3, slot] = coarse_basis[i] @ (np.roll(partner, -1) - np.roll(partner, 1))
                for j in range(4):
                    source = (2 * i + j) % 4
                    lanes[t, 4 + j, slot] = 0.25 * (coarse_basis[i] @ (restrict_z @ basis[source])) * even
                lanes[t, 8, slot] = even
    return (
        forward.reshape(8 * SPACE, NZ).astype(np.float32),
        back_coarse.reshape(4 * SPACE, NZ).astype(np.float32),
        lanes.reshape(SPACE, 16, LANES).astype(np.float32),
    )


FORWARD, BACK_COARSE, LANE_TABLE = make_tables()


def turn(a, shift):
    return pltpu.roll(a, shift % LANES, 1)


def swap_blocks(arrays):
    arrays = list(arrays)
    block = lax.broadcasted_iota(jnp.int32, arrays[0].shape, 1) // NY
    for bit in (4, 2, 1):
        low = (block // bit) % 2 == 0
        for i in range(8):
            if i & bit == 0:
                a, b = arrays[i], arrays[i + bit]
                arrays[i] = jnp.where(low, a, turn(b, NY * bit))
                arrays[i + bit] = jnp.where(low, turn(a, -NY * bit), b)
    return arrays


def along_y(a, step):
    y = lax.broadcasted_iota(jnp.int32, a.shape, 1) % NY
    upper = jnp.where(y >= NY - step, turn(a, NY - step), turn(a, -step))
    lower = jnp.where(y < step, turn(a, step - NY), turn(a, step))
    return upper, lower


def below(a):
    row = lax.broadcasted_iota(jnp.int32, a.shape, 0)
    return jnp.where(row == 0, 0.0, pltpu.roll(a, 1, 0))


def above(a):
    row = lax.broadcasted_iota(jnp.int32, a.shape, 0)
    return jnp.where(row == a.shape[0] - 1, 0.0, pltpu.roll(a, a.shape[0] - 1, 0))


def rate_of(center, x_upper, x_lower, step, second_z, first_z, ratio):
    half = 0.5 * ratio
    own = second_z - 2.0 * (mach + 1.0) - 2.0
    rates = []
    ys = [along_y(center[v], step) for v in range(NVAR)]
    for v in range(NVAR):
        rates.append(x_upper[v] + (2.0 * mach + 1.0) * x_lower[v] + ys[v][0] + ys[v][1] + own * center[v])
    divergence = (x_upper[1] - x_lower[1]) + (ys[2][0] - ys[2][1]) + first_z * turn(center[3], 64)
    rates[0] = rates[0] - divergence
    rates[1] = rates[1] - (x_upper[4] - x_lower[4])
    rates[2] = rates[2] - (ys[4][0] - ys[4][1])
    rates[3] = rates[3] - first_z * turn(center[4], 64)
    rates[4] = rates[4] - divergence
    return [half * r for r in rates]


def kernel(
    old_ref, init_ref, force_ref, owner_ref, forward_ref, back_ref, table_ref,
    ends_ref, jumps_ref,
    stacked, out1, in1, state, first, out2, in2, out3, in3, packed, gathered, fine, before,
    send1, recv1, send2, recv2, send3, recv3, send4, recv4, send5, recv5,
):
    n = lax.axis_index("cuts")
    s = lax.axis_index("space")

    barrier = pltpu.get_barrier_semaphore()

    def greet_space(k, c):
        pl.semaphore_signal(barrier, inc=1, device_id={"space": lax.rem(s + k, SPACE)}, device_id_type=MESH)
        return c

    def greet_cuts(k, c):
        pl.semaphore_signal(barrier, inc=1, device_id={"cuts": lax.rem(n + k, CUTS)}, device_id_type=MESH)
        return c

    lax.fori_loop(1, SPACE, greet_space, 0)
    lax.fori_loop(1, CUTS, greet_cuts, 0)

    stacked[0:ROWS] = old_ref[...]
    stacked[ROWS : 2 * ROWS] = force_ref[...]
    row = lax.broadcasted_iota(jnp.int32, (NY, NZ), 0)
    sums = []
    for v in range(NVAR):
        both = init_ref[2 * v * NY : (2 * v + 1) * NY] + init_ref[(2 * v + 1) * NY : (2 * v + 2) * NY]
        sums.append(both + pltpu.roll(both, NY - 1, 0))
    sums.append(jnp.zeros((NY, NZ), jnp.float32))
    for pair in range(3):
        merged = jnp.where(row % 2 == 0, sums[2 * pair], pltpu.roll(sums[2 * pair + 1], 1, 0))
        stacked[2 * ROWS + pair * NY : 2 * ROWS + (pair + 1) * NY] = merged
    stacked[2 * ROWS + 3 * NY :] = jnp.zeros((NY, NZ), jnp.float32)
    for tile in range(3):
        modes = lax.dot_general(
            forward_ref[...],
            stacked[tile * LANES : (tile + 1) * LANES],
            (((1,), (1,)), ((), ())),
            precision=HIGHEST,
            preferred_element_type=jnp.float32,
        )
        by_row = swap_blocks([modes[m * SPACE : (m + 1) * SPACE] for m in range(8)])
        for r in range(8):
            for j in range(4):
                out1[pl.ds(24 * 8 * j + 8 * tile + r, 8, stride=24), :] = by_row[r][8 * j : 8 * j + 8]

    pl.semaphore_wait(barrier, SPACE + CUTS - 2)

    def exchange(source, target, rows, send, recv):
        def piece(ref, i):
            return ref.at[pl.ds(pl.multiple_of(i * rows, 8), rows), :]

        def start(k, c):
            peer = lax.rem(s + k, SPACE)
            pltpu.make_async_remote_copy(
                piece(source, peer), piece(target, s), send.at[peer], recv.at[s],
                device_id={"space": peer}, device_id_type=MESH,
            ).start()
            return c

        def settle(k, c):
            peer = lax.rem(s + k, SPACE)
            pltpu.make_async_remote_copy(
                piece(source, peer), piece(target, peer), send.at[peer], recv.at[peer],
                device_id={"space": peer}, device_id_type=MESH,
            ).wait()
            return c

        def begin():
            lax.fori_loop(1, SPACE, start, 0)
            mine = pl.ds(pl.multiple_of(s * rows, 8), rows)
            target[mine, :] = source[mine, :]

        def finish():
            lax.fori_loop(1, SPACE, settle, 0)

        return begin, finish

    begin1, finish1 = exchange(out1, in1, 24, send1, recv1)
    begin1()
    finish1()

    table = table_ref[s]
    lane = [jnp.broadcast_to(table[i : i + 1], (SPACE, LANES)) for i in range(9)]

    def arrived(r):
        return jnp.concatenate([in1[pl.ds(24 * 8 * j + r, 8, stride=24), :] for j in range(4)], axis=0)

    def restrict_modes(t):
        return lane[4] * t + lane[5] * turn(t, 96) + lane[6] * turn(t, 64) + lane[7] * turn(t, 32)

    def restrict(q0, q1):
        t = q0 + q1
        return restrict_modes(t + turn(t, -1))

    def fine_rate(ref):
        q = [[ref[(2 * v + i) * SPACE : (2 * v + i + 1) * SPACE] for i in range(2)] for v in range(NVAR)]
        low = rate_of(
            [q[v][0] for v in range(NVAR)], [q[v][1] for v in range(NVAR)], [below(q[v][1]) for v in range(NVAR)],
            1, lane[0], lane[1], courant,
        )
        high = rate_of(
            [q[v][1] for v in range(NVAR)], [above(q[v][0]) for v in range(NVAR)], [q[v][0] for v in range(NVAR)],
            1, lane[0], lane[1], courant,
        )
        return q, [[low[v], high[v]] for v in range(NVAR)]

    def coarse_advance(c):
        r = rate_of(c, [above(a) for a in c], [below(a) for a in c], 2, lane[2], lane[3], coarse_courant)
        return [c[v] + r[v] for v in range(NVAR)]

    for r in range(2 * NVAR):
        state[r * SPACE : (r + 1) * SPACE] = arrived(r)
    place = lax.broadcasted_iota(jnp.int32, (SPACE, LANES), 0)
    hits = [(place == owner_ref[n, k]).astype(jnp.float32) for k in range(STEPS)]
    old_coarse = [restrict(arrived(2 * v), arrived(2 * v + 1)) for v in range(NVAR)]
    for k in range(STEPS):
        q, rates = fine_rate(state)
        scale = courant * hits[k]
        for v in range(NVAR):
            for i in range(2):
                at = slice((2 * v + i) * SPACE, (2 * v + i + 1) * SPACE)
                source = scale * arrived(2 * NVAR + 2 * v + i)
                first[at] = q[v][i] + rates[v][i] + source
        q1, rates1 = fine_rate(first)
        for v in range(NVAR):
            for i in range(2):
                at = slice((2 * v + i) * SPACE, (2 * v + i + 1) * SPACE)
                source = scale * arrived(2 * NVAR + 2 * v + i)
                state[at] = 0.5 * (state[at] + q1[v][i] + rates1[v][i] + source)

    final = [[state[(2 * v + i) * SPACE : (2 * v + i + 1) * SPACE] for i in range(2)] for v in range(NVAR)]
    count = hits[0] + hits[1] + hits[2]
    coarse_source = [
        courant * count * restrict(arrived(2 * NVAR + 2 * v), arrived(2 * NVAR + 2 * v + 1)) for v in range(NVAR)
    ]
    guess_old = [a + b for a, b in zip(coarse_advance(old_coarse), coarse_source)]
    for v in range(NVAR):
        gain = coarse_source[v] + restrict(final[v][0], final[v][1]) - guess_old[v]
        packed[8 * v : 8 * v + 8] = (
            gain[0:8] + turn(gain[8:16], 1) + turn(gain[16:24], 32) + turn(gain[24:32], 33)
        )

    def send_gain(k, c):
        pltpu.make_async_remote_copy(
            packed, gathered.at[n], send4.at[k], recv4.at[n], device_id={"cuts": n + k}, device_id_type=MESH
        ).start()
        return c

    def sent_gain(k, c):
        pltpu.make_async_remote_copy(
            packed, gathered.at[n], send4.at[k], recv4.at[n], device_id={"cuts": n + k}, device_id_type=MESH
        ).wait_send()
        return c

    lax.fori_loop(1, CUTS - n, send_gain, 0)

    for v in range(NVAR):
        for i in range(2):
            for j in range(4):
                out2[pl.ds(16 * 8 * j + 2 * v + i, 8, stride=16), :] = final[v][i][8 * j : 8 * j + 8]
    begin2, finish2 = exchange(out2, in2, 16, send2, recv2)
    begin2()

    useful = lane[8][0:8]

    def advance(m, c):
        pltpu.make_async_remote_copy(
            packed, gathered.at[m], send4.at[0], recv4.at[m], device_id={"cuts": m}, device_id_type=MESH
        ).wait_recv()
        moved = coarse_advance(list(c))
        result = []
        for v in range(NVAR):
            g = gathered[m, 8 * v : 8 * v + 8]
            parts = [useful * g, useful * turn(g, -1), useful * turn(g, -32), useful * turn(g, -33)]
            result.append(moved[v] + jnp.concatenate(parts, axis=0))
        return tuple(result)

    begin_coarse = []
    for v in range(NVAR):
        a = arrived(4 * NVAR + v // 2)
        begin_coarse.append(restrict_modes(turn(a, -1) if v % 2 else a))
    start = lax.fori_loop(0, n, advance, tuple(begin_coarse))
    guess_new = [a + b for a, b in zip(coarse_advance(list(start)), coarse_source)]
    for v in range(NVAR):
        change = guess_new[v] - guess_old[v]
        change = change + turn(change, 1)
        for j in range(4):
            out3[pl.ds(8 * 8 * j + v, 8, stride=8), :] = change[8 * j : 8 * j + 8]
    begin3, finish3 = exchange(out3, in3, 8, send3, recv3)
    begin3()

    finish2()
    halves = []
    for tile in range(2):
        rows = []
        for r in range(8):
            from_row = min(8 * tile + r, 2 * NVAR - 1)
            rows.append(
                jnp.concatenate([in2[pl.ds(16 * 8 * j + from_row, 8, stride=16), :] for j in range(4)], axis=0)
            )
        halves.append(jnp.concatenate(swap_blocks(rows), axis=0).T)
    modes = jnp.concatenate([halves[0], halves[1][: ROWS - LANES]], axis=0)
    fine[...] = jnp.dot(modes, forward_ref[...], precision=HIGHEST, preferred_element_type=jnp.float32)

    def to_next():
        return pltpu.make_async_remote_copy(
            fine, before, send5, recv5, device_id={"cuts": lax.rem(n + 1, CUTS)}, device_id_type=MESH
        )

    @pl.when(n < CUTS - 1)
    def _():
        to_next().start()

    finish3()
    rows = []
    for v in range(8):
        from_row = min(v, NVAR - 1)
        rows.append(jnp.concatenate([in3[pl.ds(8 * 8 * j + from_row, 8, stride=8), :] for j in range(4)], axis=0))
    by_mode = swap_blocks(rows)
    change = jnp.concatenate([by_mode[0], by_mode[1], by_mode[4], by_mode[5]], axis=0).T
    change = jnp.dot(change[: NVAR * NY], back_ref[...], precision=HIGHEST, preferred_element_type=jnp.float32)
    for v in range(NVAR):
        for i in range(2):
            at = slice((2 * v + i) * NY, (2 * v + i + 1) * NY)
            ends_ref[at] = fine[at] + change[v * NY : (v + 1) * NY]

    lax.fori_loop(1, CUTS - n, sent_gain, 0)

    @pl.when(n == 0)
    def _():
        jumps_ref[...] = old_ref[...] - init_ref[...]

    @pl.when(n > 0)
    def _():
        to_next().wait_recv()
        jumps_ref[...] = old_ref[...] - before[...]

    @pl.when(n < CUTS - 1)
    def _():
        to_next().wait_send()


def body(old_starts, initial, blade_force, blade_owner):
    vmem = pl.BlockSpec(memory_space=pltpu.VMEM)
    smem = pl.BlockSpec(memory_space=pltpu.SMEM)
    f32 = jnp.float32
    dma = pltpu.SemaphoreType.DMA
    ends, jumps = pl.pallas_call(
        kernel,
        out_shape=[jax.ShapeDtypeStruct((ROWS, NZ), f32)] * 2,
        in_specs=[vmem, vmem, vmem, smem, vmem, vmem, vmem],
        out_specs=[vmem, vmem],
        scratch_shapes=[
            pltpu.VMEM((3 * LANES, NZ), f32),
            pltpu.VMEM((SPACE * 24, LANES), f32),
            pltpu.VMEM((SPACE * 24, LANES), f32),
            pltpu.VMEM((2 * NVAR * SPACE, LANES), f32),
            pltpu.VMEM((2 * NVAR * SPACE, LANES), f32),
            pltpu.VMEM((SPACE * 16, LANES), f32),
            pltpu.VMEM((SPACE * 16, LANES), f32),
            pltpu.VMEM((SPACE * 8, LANES), f32),
            pltpu.VMEM((SPACE * 8, LANES), f32),
            pltpu.VMEM((8 * NVAR, LANES), f32),
            pltpu.VMEM((CUTS, 8 * NVAR, LANES), f32),
            pltpu.VMEM((ROWS, NZ), f32),
            pltpu.VMEM((ROWS, NZ), f32),
            dma((SPACE,)),
            dma((SPACE,)),
            dma((SPACE,)),
            dma((SPACE,)),
            dma((SPACE,)),
            dma((SPACE,)),
            dma((CUTS,)),
            dma((CUTS,)),
            dma,
            dma,
        ],
        compiler_params=pltpu.CompilerParams(
            collective_id=0, has_side_effects=True, vmem_limit_bytes=24 * 2**20
        ),
    )(
        old_starts.reshape(ROWS, NZ),
        initial.reshape(ROWS, NZ),
        blade_force.reshape(ROWS, NZ),
        blade_owner,
        jnp.asarray(FORWARD),
        jnp.asarray(BACK_COARSE),
        jnp.asarray(LANE_TABLE),
    )
    shape = old_starts.shape
    return ends.reshape(shape), jumps.reshape(shape)


def solution(mesh):
    placed = (
        P("cuts", None, "space", None, None),
        P(None, "space", None, None),
        P(None, "space", None, None),
        P(),
    )
    return jax.shard_map(
        body,
        mesh=mesh,
        in_specs=placed,
        out_specs=(P("cuts", None, "space", None, None), P("cuts", None, "space", None, None)),
        check_vma=False,
    )
```

time: 494 us -> 58.9 us (0.12)
  the two profiles are of different devices: /device:TPU:31 before, /device:TPU:19 now
where the time goes in v1:
time: 58.9 us; the launch traced here: 58.6 us
  Pallas kernels  50.3 us (85%)
  local copies, waits for them, and re-layouts  7.64 us (13%)
  between operations  0.65 us (1%)
    pallas_call x1, Pallas kernels, body(): pl.pallas_call(kernel, out_shape=[jax.ShapeDtypeStruct((ROWS, NZ), f32)]...  50.3 us
    unnamed x17, local copies, waits for them, and re-layouts  7.64 us

profile of v1, /device:TPU:19, one launch (start us, length us, event | category | flops | bytes accessed | tf_op | source)
XLA Modules:
  0.0 58.6 jit_solution(9750704529335813915)
XLA Ops:
  0.6 0.0 copy-start.6
  0.6 0.7 %copy-done.6 = s32[16,3]{0,1:T(4,128)S(1)} copy-done((s32[16,3]{0,1:T(4,128)S(1)}, s32[16,3]{0,1:T(4,128)}, u32[]{:S(2)}) %copy-start.6) | copy-done | bytes 216
  1.3 0.1 copy.9.owner_ref
  1.4 0.0 copy-start
  1.4 0.9 %copy-done = f32[32,16,128]{2,1,0:T(8,128)S(1)} copy-done((f32[32,16,128]{2,1,0:T(8,128)S(1)}, f32[32,16,128]{2,1,0:T(8,128)}, u32[]{:S(2)}) %copy-start) | copy-done | bytes 262168
  2.3 0.0 copy-start.1
  2.3 0.9 %copy-done.1 = f32[256,256]{1,0:T(8,128)S(1)} copy-done((f32[256,256]{1,0:T(8,128)S(1)}, f32[256,256]{1,0:T(8,128)}, u32[]{:S(2)}) %copy-start.1) | copy-done | bytes 262168
  3.3 0.0 copy-start.2
  3.3 0.9 %copy-done.2 = f32[1,5,2,16,256]{4,3,2,1,0:T(8,128)S(1)} copy-done((f32[1,5,2,16,256]{4,3,2,1,0:T(8,128)S(1)}, f32[1,5,2,16,256]{4,3,2,1,0:T(8,128)}, u32[]{:S(2)}) %copy-start.2) | copy-done | bytes 163864
  4.2 0.0 copy-start.3
  4.2 0.9 %copy-done.3 = f32[5,2,16,256]{3,2,1,0:T(8,128)S(1)} copy-done((f32[5,2,16,256]{3,2,1,0:T(8,128)S(1)}, f32[5,2,16,256]{3,2,1,0:T(8,128)}, u32[]{:S(2)}) %copy-start.3) | copy-done | bytes 163864
  5.1 0.0 copy-start.4
  5.1 0.9 %copy-done.4 = f32[5,2,16,256]{3,2,1,0:T(8,128)S(1)} copy-done((f32[5,2,16,256]{3,2,1,0:T(8,128)S(1)}, f32[5,2,16,256]{3,2,1,0:T(8,128)}, u32[]{:S(2)}) %copy-start.4) | copy-done | bytes 163864
  6.0 0.0 copy-start.5
  6.0 0.9 %copy-done.5 = f32[128,256]{1,0:T(8,128)S(1)} copy-done((f32[128,256]{1,0:T(8,128)S(1)}, f32[128,256]{1,0:T(8,128)}, u32[]{:S(2)}) %copy-start.5) | copy-done | bytes 131096
  7.0 50.3 %shard_map.86 = (f32[160,256]{1,0:T(8,128)S(1)}, f32[160,256]{1,0:T(8,128)S(1)}) custom-call(f32[160,256]{1,0:T(8,128)S(1)} %bitcast.5, f32[160,256]{1,0:T(8,128)S(1)} %bitcast.6, f32[160,256]{1,0:T(8,128)S(1)} %bitcast.7, s32[16,3]{1,0:T(8,128)S(1)} %copy.9.owner_ref, f32[256,256]{1,0:T(8,128)S(1)} %copy-done.1, f32[128,256]{1,0:T(8,128)S(1)} %copy-done.5, ...), custom_call_target="tpu_custom_call" | custom-call | tf_op jit(solution)/shard_map/pallas_call | solution.py:385
  57.3 0.7 %copy.12 = f32[1,5,2,16,256]{4,3,2,1,0:T(8,128)} copy(f32[1,5,2,16,256]{4,3,2,1,0:T(8,128)S(1)} %bitcast.9) | data formatting | bytes 327680
  57.9 0.7 %copy.13 = f32[1,5,2,16,256]{4,3,2,1,0:T(8,128)} copy(f32[1,5,2,16,256]{4,3,2,1,0:T(8,128)S(1)} %bitcast.8) | data formatting | bytes 327680
Async XLA Ops:
  0.6 0.7 %copy-start.6 = (s32[16,3]{0,1:T(4,128)S(1)}, s32[16,3]{0,1:T(4,128)}, u32[]{:S(2)}) copy-start(s32[16,3]{0,1:T(4,128)} %param.10) | copy-start | bytes 580
  1.4 0.9 %copy-start = (f32[32,16,128]{2,1,0:T(8,128)S(1)}, f32[32,16,128]{2,1,0:T(8,128)}, u32[]{:S(2)}) copy-start(f32[32,16,128]{2,1,0:T(8,128)} %constant.8.clone.table_ref) | copy-start | bytes 786436
  2.3 0.9 %copy-start.1 = (f32[256,256]{1,0:T(8,128)S(1)}, f32[256,256]{1,0:T(8,128)}, u32[]{:S(2)}) copy-start(f32[256,256]{1,0:T(8,128)} %constant.6.clone.forward_ref) | copy-start | bytes 786436
  3.3 0.9 %copy-start.2 = (f32[1,5,2,16,256]{4,3,2,1,0:T(8,128)S(1)}, f32[1,5,2,16,256]{4,3,2,1,0:T(8,128)}, u32[]{:S(2)}) copy-start(f32[1,5,2,16,256]{4,3,2,1,0:T(8,128)} %param.7) | copy-start | bytes 491524
  4.2 0.9 %copy-start.3 = (f32[5,2,16,256]{3,2,1,0:T(8,128)S(1)}, f32[5,2,16,256]{3,2,1,0:T(8,128)}, u32[]{:S(2)}) copy-start(f32[5,2,16,256]{3,2,1,0:T(8,128)} %param.8) | copy-start | bytes 491524
  5.1 0.9 %copy-start.4 = (f32[5,2,16,256]{3,2,1,0:T(8,128)S(1)}, f32[5,2,16,256]{3,2,1,0:T(8,128)}, u32[]{:S(2)}) copy-start(f32[5,2,16,256]{3,2,1,0:T(8,128)} %param.9) | copy-start | bytes 491524
  6.0 0.9 %copy-start.5 = (f32[128,256]{1,0:T(8,128)S(1)}, f32[128,256]{1,0:T(8,128)}, u32[]{:S(2)}) copy-start(f32[128,256]{1,0:T(8,128)} %constant.7.clone.back_ref) | copy-start | bytes 393220

commit v2 on v1

--- a/solution.py
+++ b/solution.py
@@ -134,18 +134,39 @@
 
 
 def kernel(
-    old_ref, init_ref, force_ref, owner_ref, forward_ref, back_ref, table_ref,
-    ends_ref, jumps_ref,
-    stacked, out1, in1, state, first, out2, in2, out3, in3, packed, gathered, fine, before,
-    send1, recv1, send2, recv2, send3, recv3, send4, recv4, send5, recv5,
+    old_hbm, init_hbm, force_hbm, owner_hbm, forward_hbm, back_hbm, table_hbm,
+    fine_hbm, change_hbm, before_hbm,
+    init_ref, owner_ref, forward_ref, back_ref, table, stacked, out1, in1, state, first, out2, in2, out3, in3, packed, gathered, fine, change_ref,
+    load, send1, recv1, send2, recv2, send3, recv3, send4, recv4, send5, recv5, store,
 ):
     n = lax.axis_index("cuts")
     s = lax.axis_index("space")
 
+    def peer_of(k):
+        return lax.rem(s + SPACE // 2 + (k // 2) * (1 - 2 * lax.rem(k, 2)), SPACE)
+
+    old_ref = stacked.at[0:ROWS]
+    loads = [
+        pltpu.make_async_copy(source, target, load.at[i])
+        for i, (source, target) in enumerate(
+            (
+                (forward_hbm, forward_ref),
+                (old_hbm, old_ref),
+                (force_hbm, stacked.at[ROWS : 2 * ROWS]),
+                (init_hbm, init_ref),
+                (owner_hbm, owner_ref),
+                (table_hbm.at[s], table),
+                (back_hbm, back_ref),
+            )
+        )
+    ]
+    for copy in loads:
+        copy.start()
+
     barrier = pltpu.get_barrier_semaphore()
 
     def greet_space(k, c):
-        pl.semaphore_signal(barrier, inc=1, device_id={"space": lax.rem(s + k, SPACE)}, device_id_type=MESH)
+        pl.semaphore_signal(barrier, inc=1, device_id={"space": peer_of(k)}, device_id_type=MESH)
         return c
 
     def greet_cuts(k, c):
@@ -155,8 +176,8 @@
     lax.fori_loop(1, SPACE, greet_space, 0)
     lax.fori_loop(1, CUTS, greet_cuts, 0)
 
-    stacked[0:ROWS] = old_ref[...]
-    stacked[ROWS : 2 * ROWS] = force_ref[...]
+    for copy in loads[:4]:
+        copy.wait()
     row = lax.broadcasted_iota(jnp.int32, (NY, NZ), 0)
     sums = []
     for v in range(NVAR):
@@ -187,7 +208,7 @@
             return ref.at[pl.ds(pl.multiple_of(i * rows, 8), rows), :]
 
         def start(k, c):
-            peer = lax.rem(s + k, SPACE)
+            peer = peer_of(k)
             pltpu.make_async_remote_copy(
                 piece(source, peer), piece(target, s), send.at[peer], recv.at[s],
                 device_id={"space": peer}, device_id_type=MESH,
@@ -195,7 +216,7 @@
             return c
 
         def settle(k, c):
-            peer = lax.rem(s + k, SPACE)
+            peer = peer_of(k)
             pltpu.make_async_remote_copy(
                 piece(source, peer), piece(target, peer), send.at[peer], recv.at[peer],
                 device_id={"space": peer}, device_id_type=MESH,
@@ -214,9 +235,10 @@
 
     begin1, finish1 = exchange(out1, in1, 24, send1, recv1)
     begin1()
+    for copy in loads[4:]:
+        copy.wait()
     finish1()
 
-    table = table_ref[s]
     lane = [jnp.broadcast_to(table[i : i + 1], (SPACE, LANES)) for i in range(9)]
 
     def arrived(r):
@@ -248,7 +270,7 @@
     for r in range(2 * NVAR):
         state[r * SPACE : (r + 1) * SPACE] = arrived(r)
     place = lax.broadcasted_iota(jnp.int32, (SPACE, LANES), 0)
-    hits = [(place == owner_ref[n, k]).astype(jnp.float32) for k in range(STEPS)]
+    hits = [(place == owner_ref[k, n]).astype(jnp.float32) for k in range(STEPS)]
     old_coarse = [restrict(arrived(2 * v), arrived(2 * v + 1)) for v in range(NVAR)]
     for k in range(STEPS):
         q, rates = fine_rate(state)
@@ -339,14 +361,23 @@
     modes = jnp.concatenate([halves[0], halves[1][: ROWS - LANES]], axis=0)
     fine[...] = jnp.dot(modes, forward_ref[...], precision=HIGHEST, preferred_element_type=jnp.float32)
 
+    keep_fine = pltpu.make_async_copy(fine, fine_hbm, store.at[0])
+    keep_fine.start()
     def to_next():
         return pltpu.make_async_remote_copy(
-            fine, before, send5, recv5, device_id={"cuts": lax.rem(n + 1, CUTS)}, device_id_type=MESH
-        )
+            fine, before_hbm, send5, recv5, device_id={"cuts": lax.rem(n + 1, CUTS)}, device_id_type=MESH
+        )
+
+    def keep_initial():
+        return pltpu.make_async_copy(init_ref, before_hbm, store.at[2])
 
     @pl.when(n < CUTS - 1)
     def _():
         to_next().start()
+
+    @pl.when(n == 0)
+    def _():
+        keep_initial().start()
 
     finish3()
     rows = []
@@ -355,39 +386,45 @@
         rows.append(jnp.concatenate([in3[pl.ds(8 * 8 * j + from_row, 8, stride=8), :] for j in range(4)], axis=0))
     by_mode = swap_blocks(rows)
     change = jnp.concatenate([by_mode[0], by_mode[1], by_mode[4], by_mode[5]], axis=0).T
-    change = jnp.dot(change[: NVAR * NY], back_ref[...], precision=HIGHEST, preferred_element_type=jnp.float32)
-    for v in range(NVAR):
-        for i in range(2):
-            at = slice((2 * v + i) * NY, (2 * v + i + 1) * NY)
-            ends_ref[at] = fine[at] + change[v * NY : (v + 1) * NY]
+    change_ref[...] = jnp.dot(
+        change[: NVAR * NY], back_ref[...], precision=HIGHEST, preferred_element_type=jnp.float32
+    )
+    keep_change = pltpu.make_async_copy(change_ref, change_hbm, store.at[1])
+    keep_change.start()
 
     lax.fori_loop(1, CUTS - n, sent_gain, 0)
-
-    @pl.when(n == 0)
-    def _():
-        jumps_ref[...] = old_ref[...] - init_ref[...]
+    keep_fine.wait()
 
     @pl.when(n > 0)
     def _():
         to_next().wait_recv()
-        jumps_ref[...] = old_ref[...] - before[...]
 
     @pl.when(n < CUTS - 1)
     def _():
         to_next().wait_send()
 
+    @pl.when(n == 0)
+    def _():
+        keep_initial().wait()
+
+    keep_change.wait()
+
 
 def body(old_starts, initial, blade_force, blade_owner):
-    vmem = pl.BlockSpec(memory_space=pltpu.VMEM)
-    smem = pl.BlockSpec(memory_space=pltpu.SMEM)
+    hbm = pl.BlockSpec(memory_space=pl.ANY)
     f32 = jnp.float32
     dma = pltpu.SemaphoreType.DMA
-    ends, jumps = pl.pallas_call(
+    fine, change, before = pl.pallas_call(
         kernel,
-        out_shape=[jax.ShapeDtypeStruct((ROWS, NZ), f32)] * 2,
-        in_specs=[vmem, vmem, vmem, smem, vmem, vmem, vmem],
-        out_specs=[vmem, vmem],
+        out_shape=[jax.ShapeDtypeStruct((rows, NZ), f32) for rows in (ROWS, NVAR * NY, ROWS)],
+        in_specs=[hbm] * 7,
+        out_specs=[hbm] * 3,
         scratch_shapes=[
+            pltpu.VMEM((ROWS, NZ), f32),
+            pltpu.SMEM((STEPS, CUTS), jnp.int32),
+            pltpu.VMEM((NZ, NZ), f32),
+            pltpu.VMEM((NZ // 2, NZ), f32),
+            pltpu.VMEM((16, LANES), f32),
             pltpu.VMEM((3 * LANES, NZ), f32),
             pltpu.VMEM((SPACE * 24, LANES), f32),
             pltpu.VMEM((SPACE * 24, LANES), f32),
@@ -400,7 +437,8 @@
             pltpu.VMEM((8 * NVAR, LANES), f32),
             pltpu.VMEM((CUTS, 8 * NVAR, LANES), f32),
             pltpu.VMEM((ROWS, NZ), f32),
-            pltpu.VMEM((ROWS, NZ), f32),
+            pltpu.VMEM((NVAR * NY, NZ), f32),
+            dma((7,)),
             dma((SPACE,)),
             dma((SPACE,)),
             dma((SPACE,)),
@@ -411,21 +449,23 @@
             dma((CUTS,)),
             dma,
             dma,
+            dma((3,)),
         ],
         compiler_params=pltpu.CompilerParams(
-            collective_id=0, has_side_effects=True, vmem_limit_bytes=24 * 2**20
+            collective_id=0, has_side_effects=True, vmem_limit_bytes=56 * 2**20
         ),
     )(
         old_starts.reshape(ROWS, NZ),
         initial.reshape(ROWS, NZ),
         blade_force.reshape(ROWS, NZ),
-        blade_owner,
+        blade_owner.T,
         jnp.asarray(FORWARD),
         jnp.asarray(BACK_COARSE),
         jnp.asarray(LANE_TABLE),
     )
     shape = old_starts.shape
-    return ends.reshape(shape), jumps.reshape(shape)
+    ends = fine.reshape(shape) + change.reshape(1, NVAR, 1, NY, NZ)
+    return ends, old_starts - before.reshape(shape)
 
 
 def solution(mesh):

time: 58.9 us -> 52.4 us (0.89)
  the two profiles are of different devices: /device:TPU:19 before, /device:TPU:2 now
where the time goes in v2:
time: 52.4 us; the launch traced here: 52.3 us
  Pallas kernels  49.2 us (94%)
  other arithmetic  2.38 us (5%)
  between operations  0.66 us (1%)
    pallas_call x1, Pallas kernels, body(): pl.pallas_call(kernel, out_shape=[jax.ShapeDtypeStruct((rows, NZ), f32) f...  49.2 us
    add x1, other arithmetic, body(): ends = fine.reshape(shape) + change.reshape(1, NVAR, 1, NY, NZ)  1.69 us

profile of v2, /device:TPU:2, one launch (start us, length us, event | category | flops | bytes accessed | tf_op | source)
XLA Modules:
  0.0 52.3 jit_solution(1294067795068812283)
XLA Ops:
  0.6 49.2 %shard_map.86 = (f32[160,256]{1,0:T(8,128)}, f32[80,256]{1,0:T(8,128)}, f32[160,256]{1,0:T(8,128)}) custom-call(f32[160,256]{1,0:T(8,128)} %bitcast.7, f32[160,256]{1,0:T(8,128)} %bitcast.8, f32[160,256]{1,0:T(8,128)} %bitcast.9, s32[3,16]{1,0:T(4,128)} %bitcast.13, f32[256,256]{1,0:T(8,128)} %constant.6.clone.forward_hbm, ...), custom_call_target="tpu_custom_call" | custom-call | tf_op jit(solution)/shard_map/pallas_call | solution.py:417
  49.9 0.0 copy-start
  49.9 0.0 copy-start.1
  49.9 1.7 %broadcast_add_fusion = f32[1,5,2,16,256]{4,3,2,1,0:T(8,128)} fusion(f32[1,5,2,16,256]{4,3,2,1,0:T(8,128)} %bitcast.10, f32[5,16,256]{2,1,0:T(8,128)} %bitcast.12), kind=kLoop, calls=%fused_computation | loop fusion | flops 40960 | bytes 409600 | tf_op jit(solution)/shard_map/add | solution.py:467
  51.6 0.0 copy-done
  51.6 0.0 copy-done.1
  51.6 0.7 %sub.3 = f32[1,5,2,16,256]{4,3,2,1,0:T(8,128)} subtract(f32[1,5,2,16,256]{4,3,2,1,0:T(8,128)S(1)} %copy-done, f32[1,5,2,16,256]{4,3,2,1,0:T(8,128)S(1)} %bitcast.11) | non-fusion elementwise | flops 40960 | bytes 491520 | tf_op jit(solution)/shard_map/sub | solution.py:468
Async XLA Ops:
  49.9 1.7 %copy-start = (f32[1,5,2,16,256]{4,3,2,1,0:T(8,128)S(1)}, f32[1,5,2,16,256]{4,3,2,1,0:T(8,128)}, u32[]{:S(2)}) copy-start(f32[1,5,2,16,256]{4,3,2,1,0:T(8,128)} %param.7) | copy-start | bytes 491524
  49.9 1.7 %copy-start.1 = (f32[160,256]{1,0:T(8,128)S(1)}, f32[160,256]{1,0:T(8,128)}, u32[]{:S(2)}) copy-start(f32[160,256]{1,0:T(8,128)} %get-tuple-element.7) | copy-start | bytes 491524

commit v3 on v2

--- a/solution.py
+++ b/solution.py
@@ -81,6 +81,23 @@
 
 
 FORWARD, BACK_COARSE, LANE_TABLE = make_tables()
+GATHER_ORDER = (12, 4, 11, 13, 3, 5, 10, 14, 2, 6, 9, 15, 1, 7, 8)
+
+
+def in_two(a):
+    high = a.astype(jnp.bfloat16)
+    return high, (a - high.astype(jnp.float32)).astype(jnp.bfloat16)
+
+
+def stack_table(a):
+    high = a.astype(jnp.bfloat16)
+    low = (a - high.astype(np.float32)).astype(jnp.bfloat16)
+    return np.concatenate([high, high, low], axis=0)
+
+
+def times_table(a, table):
+    high, low = in_two(a)
+    return jnp.dot(jnp.concatenate([high, low, high], axis=1), table, preferred_element_type=jnp.float32)
 
 
 def turn(a, shift):
@@ -134,9 +151,9 @@
 
 
 def kernel(
-    old_hbm, init_hbm, force_hbm, owner_hbm, forward_hbm, back_hbm, table_hbm,
-    fine_hbm, change_hbm, before_hbm,
-    init_ref, owner_ref, forward_ref, back_ref, table, stacked, out1, in1, state, first, out2, in2, out3, in3, packed, gathered, fine, change_ref,
+    old_hbm, init_hbm, force_hbm, owner_hbm, forward_hbm, inverse_hbm, back_hbm, table_hbm,
+    ends_hbm, before_hbm,
+    init_ref, owner_ref, forward_ref, inverse_ref, back_ref, table, stacked, out1, in1, state, first, out2, in2, out3, in3, packed, gathered, fine, ends,
     load, send1, recv1, send2, recv2, send3, recv3, send4, recv4, send5, recv5, store,
 ):
     n = lax.axis_index("cuts")
@@ -157,6 +174,7 @@
                 (owner_hbm, owner_ref),
                 (table_hbm.at[s], table),
                 (back_hbm, back_ref),
+                (inverse_hbm, inverse_ref),
             )
         )
     ]
@@ -205,31 +223,31 @@
 
     def exchange(source, target, rows, send, recv):
         def piece(ref, i):
+            if rows is None:
+                return ref.at[i]
             return ref.at[pl.ds(pl.multiple_of(i * rows, 8), rows), :]
 
         def start(k, c):
             peer = peer_of(k)
             pltpu.make_async_remote_copy(
-                piece(source, peer), piece(target, s), send.at[peer], recv.at[s],
+                piece(source, peer), piece(target, s), send, recv,
                 device_id={"space": peer}, device_id_type=MESH,
             ).start()
             return c
 
-        def settle(k, c):
-            peer = peer_of(k)
+        def begin():
+            lax.fori_loop(1, SPACE, start, 0, unroll=True)
+            if rows is None:
+                target[s] = source[s]
+            else:
+                mine = pl.ds(pl.multiple_of(s * rows, 8), rows)
+                target[mine, :] = source[mine, :]
+
+        def finish():
+            others = pl.ds(0, (SPACE - 1) * (rows or 1))
             pltpu.make_async_remote_copy(
-                piece(source, peer), piece(target, peer), send.at[peer], recv.at[peer],
-                device_id={"space": peer}, device_id_type=MESH,
+                source.at[others], target.at[others], send, recv, device_id={"space": peer_of(1)}, device_id_type=MESH
             ).wait()
-            return c
-
-        def begin():
-            lax.fori_loop(1, SPACE, start, 0)
-            mine = pl.ds(pl.multiple_of(s * rows, 8), rows)
-            target[mine, :] = source[mine, :]
-
-        def finish():
-            lax.fori_loop(1, SPACE, settle, 0)
 
         return begin, finish
 
@@ -299,25 +317,20 @@
             gain[0:8] + turn(gain[8:16], 1) + turn(gain[16:24], 32) + turn(gain[24:32], 33)
         )
 
-    def send_gain(k, c):
-        pltpu.make_async_remote_copy(
+    def send_gain(k):
+        return pltpu.make_async_remote_copy(
             packed, gathered.at[n], send4.at[k], recv4.at[n], device_id={"cuts": n + k}, device_id_type=MESH
-        ).start()
-        return c
-
-    def sent_gain(k, c):
-        pltpu.make_async_remote_copy(
-            packed, gathered.at[n], send4.at[k], recv4.at[n], device_id={"cuts": n + k}, device_id_type=MESH
-        ).wait_send()
-        return c
-
-    lax.fori_loop(1, CUTS - n, send_gain, 0)
+        )
+
+    for k in GATHER_ORDER:
+        @pl.when(n + k < CUTS)
+        def _():
+            send_gain(k).start()
 
     for v in range(NVAR):
         for i in range(2):
-            for j in range(4):
-                out2[pl.ds(16 * 8 * j + 2 * v + i, 8, stride=16), :] = final[v][i][8 * j : 8 * j + 8]
-    begin2, finish2 = exchange(out2, in2, 16, send2, recv2)
+            out2[:, v, i, :] = final[v][i]
+    begin2, finish2 = exchange(out2, in2, None, send2, recv2)
     begin2()
 
     useful = lane[8][0:8]
@@ -340,12 +353,10 @@
         begin_coarse.append(restrict_modes(turn(a, -1) if v % 2 else a))
     start = lax.fori_loop(0, n, advance, tuple(begin_coarse))
     guess_new = [a + b for a, b in zip(coarse_advance(list(start)), coarse_source)]
-    for v in range(NVAR):
-        change = guess_new[v] - guess_old[v]
-        change = change + turn(change, 1)
-        for j in range(4):
-            out3[pl.ds(8 * 8 * j + v, 8, stride=8), :] = change[8 * j : 8 * j + 8]
-    begin3, finish3 = exchange(out3, in3, 8, send3, recv3)
+    change = [guess_new[v] - guess_old[v] for v in range(NVAR)]
+    out3[:, 0, :] = change[0] + turn(change[1], 1) + turn(change[2], 32) + turn(change[3], 33)
+    out3[:, 1, :] = change[4]
+    begin3, finish3 = exchange(out3, in3, None, send3, recv3)
     begin3()
 
     finish2()
@@ -354,22 +365,18 @@
         rows = []
         for r in range(8):
             from_row = min(8 * tile + r, 2 * NVAR - 1)
-            rows.append(
-                jnp.concatenate([in2[pl.ds(16 * 8 * j + from_row, 8, stride=16), :] for j in range(4)], axis=0)
-            )
+            rows.append(in2[:, from_row // 2, from_row % 2, :])
         halves.append(jnp.concatenate(swap_blocks(rows), axis=0).T)
     modes = jnp.concatenate([halves[0], halves[1][: ROWS - LANES]], axis=0)
-    fine[...] = jnp.dot(modes, forward_ref[...], precision=HIGHEST, preferred_element_type=jnp.float32)
-
-    keep_fine = pltpu.make_async_copy(fine, fine_hbm, store.at[0])
-    keep_fine.start()
+    fine[...] = times_table(modes, inverse_ref[...])
+
     def to_next():
         return pltpu.make_async_remote_copy(
             fine, before_hbm, send5, recv5, device_id={"cuts": lax.rem(n + 1, CUTS)}, device_id_type=MESH
         )
 
     def keep_initial():
-        return pltpu.make_async_copy(init_ref, before_hbm, store.at[2])
+        return pltpu.make_async_copy(init_ref, before_hbm, store.at[1])
 
     @pl.when(n < CUTS - 1)
     def _():
@@ -380,20 +387,25 @@
         keep_initial().start()
 
     finish3()
-    rows = []
-    for v in range(8):
-        from_row = min(v, NVAR - 1)
-        rows.append(jnp.concatenate([in3[pl.ds(8 * 8 * j + from_row, 8, stride=8), :] for j in range(4)], axis=0))
-    by_mode = swap_blocks(rows)
+    mask = jnp.broadcast_to(useful[0:1], (SPACE, LANES))
+    four = in3[:, 0, :]
+    rows = [mask * a for a in (four, turn(four, -1), turn(four, -32), turn(four, -33))] + [in3[:, 1, :]]
+    rows = [a + turn(a, 1) for a in rows]
+    by_mode = swap_blocks(rows + rows[4:] * 3)
     change = jnp.concatenate([by_mode[0], by_mode[1], by_mode[4], by_mode[5]], axis=0).T
-    change_ref[...] = jnp.dot(
-        change[: NVAR * NY], back_ref[...], precision=HIGHEST, preferred_element_type=jnp.float32
-    )
-    keep_change = pltpu.make_async_copy(change_ref, change_hbm, store.at[1])
-    keep_change.start()
+    change = times_table(change[: NVAR * NY], back_ref[...])
+    for v in range(NVAR):
+        for i in range(2):
+            at = slice((2 * v + i) * NY, (2 * v + i + 1) * NY)
+            ends[at] = fine[at] + change[v * NY : (v + 1) * NY]
+    keep_ends = pltpu.make_async_copy(ends, ends_hbm, store.at[0])
+    keep_ends.start()
+
+    def sent_gain(k, c):
+        send_gain(k).wait_send()
+        return c
 
     lax.fori_loop(1, CUTS - n, sent_gain, 0)
-    keep_fine.wait()
 
     @pl.when(n > 0)
     def _():
@@ -407,49 +419,50 @@
     def _():
         keep_initial().wait()
 
-    keep_change.wait()
+    keep_ends.wait()
 
 
 def body(old_starts, initial, blade_force, blade_owner):
     hbm = pl.BlockSpec(memory_space=pl.ANY)
     f32 = jnp.float32
     dma = pltpu.SemaphoreType.DMA
-    fine, change, before = pl.pallas_call(
+    ends, before = pl.pallas_call(
         kernel,
-        out_shape=[jax.ShapeDtypeStruct((rows, NZ), f32) for rows in (ROWS, NVAR * NY, ROWS)],
-        in_specs=[hbm] * 7,
-        out_specs=[hbm] * 3,
+        out_shape=[jax.ShapeDtypeStruct((rows, NZ), f32) for rows in (ROWS, ROWS)],
+        in_specs=[hbm] * 8,
+        out_specs=[hbm] * 2,
         scratch_shapes=[
             pltpu.VMEM((ROWS, NZ), f32),
             pltpu.SMEM((STEPS, CUTS), jnp.int32),
             pltpu.VMEM((NZ, NZ), f32),
-            pltpu.VMEM((NZ // 2, NZ), f32),
+            pltpu.VMEM((3 * NZ, NZ), jnp.bfloat16),
+            pltpu.VMEM((3 * NZ // 2, NZ), jnp.bfloat16),
             pltpu.VMEM((16, LANES), f32),
             pltpu.VMEM((3 * LANES, NZ), f32),
             pltpu.VMEM((SPACE * 24, LANES), f32),
             pltpu.VMEM((SPACE * 24, LANES), f32),
             pltpu.VMEM((2 * NVAR * SPACE, LANES), f32),
             pltpu.VMEM((2 * NVAR * SPACE, LANES), f32),
-            pltpu.VMEM((SPACE * 16, LANES), f32),
-            pltpu.VMEM((SPACE * 16, LANES), f32),
-            pltpu.VMEM((SPACE * 8, LANES), f32),
-            pltpu.VMEM((SPACE * 8, LANES), f32),
+            pltpu.VMEM((SPACE, NVAR, 2, LANES), f32),
+            pltpu.VMEM((SPACE, NVAR, 2, LANES), f32),
+            pltpu.VMEM((SPACE, 2, LANES), f32),
+            pltpu.VMEM((SPACE, 2, LANES), f32),
             pltpu.VMEM((8 * NVAR, LANES), f32),
             pltpu.VMEM((CUTS, 8 * NVAR, LANES), f32),
             pltpu.VMEM((ROWS, NZ), f32),
-            pltpu.VMEM((NVAR * NY, NZ), f32),
-            dma((7,)),
-            dma((SPACE,)),
-            dma((SPACE,)),
-            dma((SPACE,)),
-            dma((SPACE,)),
-            dma((SPACE,)),
-            dma((SPACE,)),
+            pltpu.VMEM((ROWS, NZ), f32),
+            dma((8,)),
+            dma,
+            dma,
+            dma,
+            dma,
+            dma,
+            dma,
             dma((CUTS,)),
             dma((CUTS,)),
             dma,
             dma,
-            dma((3,)),
+            dma((2,)),
         ],
         compiler_params=pltpu.CompilerParams(
             collective_id=0, has_side_effects=True, vmem_limit_bytes=56 * 2**20
@@ -460,12 +473,12 @@
         blade_force.reshape(ROWS, NZ),
         blade_owner.T,
         jnp.asarray(FORWARD),
-        jnp.asarray(BACK_COARSE),
+        jnp.asarray(stack_table(FORWARD)),
+        jnp.asarray(stack_table(BACK_COARSE)),
         jnp.asarray(LANE_TABLE),
     )
     shape = old_starts.shape
-    ends = fine.reshape(shape) + change.reshape(1, NVAR, 1, NY, NZ)
-    return ends, old_starts - before.reshape(shape)
+    return ends.reshape(shape), old_starts - before.reshape(shape)
 
 
 def solution(mesh):

time: 52.4 us -> 48 us (0.916)
  Pallas kernels: 49.2 us -> 44.8 us
  other arithmetic: 2.38 us -> 1.64 us
  local copies, waits for them, and re-layouts: 0.01 us -> 0.67 us
    pallas_call x1, Pallas kernels: 49.2 us -> 44.8 us  [body(): pl.pallas_call(kernel, out_shape=[jax.ShapeDtypeStruct((rows, NZ), f32) f...]
    add x1 -> x0, other arithmetic: 1.69 us -> none  [body(): ends = fine.reshape(shape) + change.reshape(1, NVAR, 1, NY, NZ)]
    sub x1, other arithmetic: 0.69 us -> 1.64 us  [body(): return (ends.reshape(shape), old_starts - before.reshape(shape))]
    unnamed x4 -> x5, local copies, waits for them, and re-layouts: 0.01 us -> 0.67 us
where the time goes in v3:
time: 48 us; the launch traced here: 47.8 us
  Pallas kernels  44.8 us (93%)
  other arithmetic  1.64 us (3%)
  local copies, waits for them, and re-layouts  0.67 us (1%)
  between operations  0.66 us (1%)
    pallas_call x1, Pallas kernels, body(): pl.pallas_call(kernel, out_shape=[jax.ShapeDtypeStruct((rows, NZ), f32) f...  44.8 us
    sub x1, other arithmetic, body(): return (ends.reshape(shape), old_starts - before.reshape(shape))  1.64 us

profile of v3, /device:TPU:2, one launch (start us, length us, event | category | flops | bytes accessed | tf_op | source)
XLA Modules:
  0.0 47.8 jit_solution(702689998004348880)
XLA Ops:
  0.6 0.0 copy-start
  0.6 44.8 %shard_map.95 = (f32[160,256]{1,0:T(8,128)}, f32[160,256]{1,0:T(8,128)}) custom-call(f32[160,256]{1,0:T(8,128)} %bitcast.6, f32[160,256]{1,0:T(8,128)} %bitcast.7, f32[160,256]{1,0:T(8,128)} %bitcast.8, s32[3,16]{1,0:T(4,128)} %bitcast.11, f32[256,256]{1,0:T(8,128)} %constant.8.clone.forward_hbm, bf16[768,256]{1,0:T(8,128)(2,1)} %constant.9.clone.inverse_hbm, ...), custom_call_target="tpu_custom_call" | custom-call | tf_op jit(solution)/shard_map/pallas_call | solution.py:429
  45.5 0.0 copy-done
  45.5 0.0 copy-start.1
  45.5 1.6 %sub.3 = f32[1,5,2,16,256]{4,3,2,1,0:T(8,128)} subtract(f32[1,5,2,16,256]{4,3,2,1,0:T(8,128)S(1)} %copy-done, f32[1,5,2,16,256]{4,3,2,1,0:T(8,128)} %bitcast.10) | non-fusion elementwise | flops 40960 | bytes 491520 | tf_op jit(solution)/shard_map/sub | solution.py:481
  47.2 0.0 copy-done.1
  47.2 0.7 %copy.11 = f32[1,5,2,16,256]{4,3,2,1,0:T(8,128)} copy(f32[1,5,2,16,256]{4,3,2,1,0:T(8,128)S(1)} %bitcast.9) | data formatting | bytes 327680
Async XLA Ops:
  0.6 44.9 %copy-start = (f32[1,5,2,16,256]{4,3,2,1,0:T(8,128)S(1)}, f32[1,5,2,16,256]{4,3,2,1,0:T(8,128)}, u32[]{:S(2)}) copy-start(f32[1,5,2,16,256]{4,3,2,1,0:T(8,128)} %param.8) | copy-start | bytes 491524
  45.5 1.7 %copy-start.1 = (f32[160,256]{1,0:T(8,128)S(1)}, f32[160,256]{1,0:T(8,128)}, u32[]{:S(2)}) copy-start(f32[160,256]{1,0:T(8,128)} %get-tuple-element.4) | copy-start | bytes 491524

commit v4 on v3

--- a/solution.py
+++ b/solution.py
@@ -9,7 +9,6 @@
 from jax.sharding import PartitionSpec as P
 
 MESH = pl.DeviceIdType.MESH
-HIGHEST = lax.Precision.HIGHEST
 
 STEPS = 3
 NVAR = 5
@@ -81,7 +80,7 @@
 
 
 FORWARD, BACK_COARSE, LANE_TABLE = make_tables()
-GATHER_ORDER = (12, 4, 11, 13, 3, 5, 10, 14, 2, 6, 9, 15, 1, 7, 8)
+GATHER_ORDER = (12, 13, 11, 14, 10, 15, 9, 8, 7, 6, 5, 4, 3, 2, 1)
 
 
 def in_two(a):
@@ -153,8 +152,8 @@
 def kernel(
     old_hbm, init_hbm, force_hbm, owner_hbm, forward_hbm, inverse_hbm, back_hbm, table_hbm,
     ends_hbm, before_hbm,
-    init_ref, owner_ref, forward_ref, inverse_ref, back_ref, table, stacked, out1, in1, state, first, out2, in2, out3, in3, packed, gathered, fine, ends,
-    load, send1, recv1, send2, recv2, send3, recv3, send4, recv4, send5, recv5, store,
+    init_ref, owner_ref, forward_ref, inverse_ref, back_ref, table, stacked, out1, in1, state, first, out2, in2, out3, in3, out6, in6, packed, gathered, fine, ends,
+    load, send1, recv1, send2, recv2, send3, recv3, send4, recv4, send5, recv5, send6, recv6, store,
 ):
     n = lax.axis_index("cuts")
     s = lax.axis_index("space")
@@ -178,9 +177,6 @@
             )
         )
     ]
-    for copy in loads:
-        copy.start()
-
     barrier = pltpu.get_barrier_semaphore()
 
     def greet_space(k, c):
@@ -191,8 +187,11 @@
         pl.semaphore_signal(barrier, inc=1, device_id={"cuts": lax.rem(n + k, CUTS)}, device_id_type=MESH)
         return c
 
-    lax.fori_loop(1, SPACE, greet_space, 0)
-    lax.fori_loop(1, CUTS, greet_cuts, 0)
+    lax.fori_loop(1, SPACE, greet_space, 0, unroll=True)
+    lax.fori_loop(1, CUTS, greet_cuts, 0, unroll=True)
+
+    for copy in loads:
+        copy.start()
 
     for copy in loads[:4]:
         copy.wait()
@@ -207,52 +206,47 @@
         stacked[2 * ROWS + pair * NY : 2 * ROWS + (pair + 1) * NY] = merged
     stacked[2 * ROWS + 3 * NY :] = jnp.zeros((NY, NZ), jnp.float32)
     for tile in range(3):
+        high, low = in_two(stacked[tile * LANES : (tile + 1) * LANES])
         modes = lax.dot_general(
             forward_ref[...],
-            stacked[tile * LANES : (tile + 1) * LANES],
+            jnp.concatenate([high, low, high], axis=1),
             (((1,), (1,)), ((), ())),
-            precision=HIGHEST,
             preferred_element_type=jnp.float32,
         )
         by_row = swap_blocks([modes[m * SPACE : (m + 1) * SPACE] for m in range(8)])
         for r in range(8):
-            for j in range(4):
-                out1[pl.ds(24 * 8 * j + 8 * tile + r, 8, stride=24), :] = by_row[r][8 * j : 8 * j + 8]
+            at = 8 * tile + r
+            if at < 4 * NVAR:
+                out1[:, at // 2, at % 2, :] = by_row[r]
+            else:
+                out6[:, at // 2 - 2 * NVAR, at % 2, :] = by_row[r]
 
     pl.semaphore_wait(barrier, SPACE + CUTS - 2)
 
-    def exchange(source, target, rows, send, recv):
-        def piece(ref, i):
-            if rows is None:
-                return ref.at[i]
-            return ref.at[pl.ds(pl.multiple_of(i * rows, 8), rows), :]
-
+    def exchange(source, target, send, recv):
         def start(k, c):
             peer = peer_of(k)
             pltpu.make_async_remote_copy(
-                piece(source, peer), piece(target, s), send, recv,
-                device_id={"space": peer}, device_id_type=MESH,
+                source.at[peer], target.at[s], send, recv, device_id={"space": peer}, device_id_type=MESH
             ).start()
             return c
 
         def begin():
             lax.fori_loop(1, SPACE, start, 0, unroll=True)
-            if rows is None:
-                target[s] = source[s]
-            else:
-                mine = pl.ds(pl.multiple_of(s * rows, 8), rows)
-                target[mine, :] = source[mine, :]
+            target[s] = source[s]
 
         def finish():
-            others = pl.ds(0, (SPACE - 1) * (rows or 1))
+            others = pl.ds(0, SPACE - 1)
             pltpu.make_async_remote_copy(
                 source.at[others], target.at[others], send, recv, device_id={"space": peer_of(1)}, device_id_type=MESH
             ).wait()
 
         return begin, finish
 
-    begin1, finish1 = exchange(out1, in1, 24, send1, recv1)
+    begin1, finish1 = exchange(out1, in1, send1, recv1)
+    begin6, finish6 = exchange(out6, in6, send6, recv6)
     begin1()
+    begin6()
     for copy in loads[4:]:
         copy.wait()
     finish1()
@@ -260,7 +254,9 @@
     lane = [jnp.broadcast_to(table[i : i + 1], (SPACE, LANES)) for i in range(9)]
 
     def arrived(r):
-        return jnp.concatenate([in1[pl.ds(24 * 8 * j + r, 8, stride=24), :] for j in range(4)], axis=0)
+        if r < 4 * NVAR:
+            return in1[:, r // 2, r % 2, :]
+        return in6[:, r // 2 - 2 * NVAR, r % 2, :]
 
     def restrict_modes(t):
         return lane[4] * t + lane[5] * turn(t, 96) + lane[6] * turn(t, 64) + lane[7] * turn(t, 32)
@@ -330,7 +326,7 @@
     for v in range(NVAR):
         for i in range(2):
             out2[:, v, i, :] = final[v][i]
-    begin2, finish2 = exchange(out2, in2, None, send2, recv2)
+    begin2, finish2 = exchange(out2, in2, send2, recv2)
     begin2()
 
     useful = lane[8][0:8]
@@ -347,6 +343,7 @@
             result.append(moved[v] + jnp.concatenate(parts, axis=0))
         return tuple(result)
 
+    finish6()
     begin_coarse = []
     for v in range(NVAR):
         a = arrived(4 * NVAR + v // 2)
@@ -356,7 +353,7 @@
     change = [guess_new[v] - guess_old[v] for v in range(NVAR)]
     out3[:, 0, :] = change[0] + turn(change[1], 1) + turn(change[2], 32) + turn(change[3], 33)
     out3[:, 1, :] = change[4]
-    begin3, finish3 = exchange(out3, in3, None, send3, recv3)
+    begin3, finish3 = exchange(out3, in3, send3, recv3)
     begin3()
 
     finish2()
@@ -434,19 +431,21 @@
         scratch_shapes=[
             pltpu.VMEM((ROWS, NZ), f32),
             pltpu.SMEM((STEPS, CUTS), jnp.int32),
-            pltpu.VMEM((NZ, NZ), f32),
+            pltpu.VMEM((NZ, 3 * NZ), jnp.bfloat16),
             pltpu.VMEM((3 * NZ, NZ), jnp.bfloat16),
             pltpu.VMEM((3 * NZ // 2, NZ), jnp.bfloat16),
             pltpu.VMEM((16, LANES), f32),
             pltpu.VMEM((3 * LANES, NZ), f32),
-            pltpu.VMEM((SPACE * 24, LANES), f32),
-            pltpu.VMEM((SPACE * 24, LANES), f32),
+            pltpu.VMEM((SPACE, 2 * NVAR, 2, LANES), f32),
+            pltpu.VMEM((SPACE, 2 * NVAR, 2, LANES), f32),
             pltpu.VMEM((2 * NVAR * SPACE, LANES), f32),
             pltpu.VMEM((2 * NVAR * SPACE, LANES), f32),
             pltpu.VMEM((SPACE, NVAR, 2, LANES), f32),
             pltpu.VMEM((SPACE, NVAR, 2, LANES), f32),
             pltpu.VMEM((SPACE, 2, LANES), f32),
             pltpu.VMEM((SPACE, 2, LANES), f32),
+            pltpu.VMEM((SPACE, 2, 2, LANES), f32),
+            pltpu.VMEM((SPACE, 2, 2, LANES), f32),
             pltpu.VMEM((8 * NVAR, LANES), f32),
             pltpu.VMEM((CUTS, 8 * NVAR, LANES), f32),
             pltpu.VMEM((ROWS, NZ), f32),
@@ -460,6 +459,8 @@
             dma,
             dma((CUTS,)),
             dma((CUTS,)),
+            dma,
+            dma,
             dma,
             dma,
             dma((2,)),
@@ -472,7 +473,7 @@
         initial.reshape(ROWS, NZ),
         blade_force.reshape(ROWS, NZ),
         blade_owner.T,
-        jnp.asarray(FORWARD),
+        jnp.asarray(np.ascontiguousarray(stack_table(FORWARD.T).T)),
         jnp.asarray(stack_table(FORWARD)),
         jnp.asarray(stack_table(BACK_COARSE)),
         jnp.asarray(LANE_TABLE),

time: 48 us -> 47 us (0.979)
  Pallas kernels: 44.8 us -> 43.9 us
    pallas_call x1, Pallas kernels: 44.8 us -> 43.9 us  [body(): pl.pallas_call(kernel, out_shape=[jax.ShapeDtypeStruct((rows, NZ), f32) f...]
where the time goes in v4:
time: 47 us; the launch traced here: 46.9 us
  Pallas kernels  43.9 us (93%)
  other arithmetic  1.64 us (3%)
  local copies, waits for them, and re-layouts  0.67 us (1%)
  between operations  0.66 us (1%)
    pallas_call x1, Pallas kernels, body(): pl.pallas_call(kernel, out_shape=[jax.ShapeDtypeStruct((rows, NZ), f32) f...  43.9 us
    sub x1, other arithmetic, body(): return (ends.reshape(shape), old_starts - before.reshape(shape))  1.64 us

profile of v4, /device:TPU:2, one launch (start us, length us, event | category | flops | bytes accessed | tf_op | source)
XLA Modules:
  0.0 46.9 jit_solution(17507263692301480589)
XLA Ops:
  0.6 0.0 copy-start
  0.6 43.9 %shard_map.95 = (f32[160,256]{1,0:T(8,128)}, f32[160,256]{1,0:T(8,128)}) custom-call(f32[160,256]{1,0:T(8,128)} %bitcast.6, f32[160,256]{1,0:T(8,128)} %bitcast.9, f32[160,256]{1,0:T(8,128)} %bitcast.10, s32[3,16]{1,0:T(4,128)} %bitcast.11, bf16[256,768]{1,0:T(8,128)(2,1)} %constant.8.clone.forward_hbm, bf16[768,256]{1,0:T(8,128)(2,1)} %constant.9.clone.inverse_hbm, ...), custom_call_target="tpu_custom_call" | custom-call | tf_op jit(solution)/shard_map/pallas_call | solution.py:426
  44.5 0.0 copy-done
  44.5 0.0 copy-start.1
  44.5 1.6 %sub.3 = f32[1,5,2,16,256]{4,3,2,1,0:T(8,128)} subtract(f32[1,5,2,16,256]{4,3,2,1,0:T(8,128)S(1)} %copy-done, f32[1,5,2,16,256]{4,3,2,1,0:T(8,128)} %bitcast.8) | non-fusion elementwise | flops 40960 | bytes 491520 | tf_op jit(solution)/shard_map/sub | solution.py:482
  46.2 0.0 copy-done.1
  46.2 0.7 %copy.11 = f32[1,5,2,16,256]{4,3,2,1,0:T(8,128)} copy(f32[1,5,2,16,256]{4,3,2,1,0:T(8,128)S(1)} %bitcast.7) | data formatting | bytes 327680
Async XLA Ops:
  0.6 43.9 %copy-start = (f32[1,5,2,16,256]{4,3,2,1,0:T(8,128)S(1)}, f32[1,5,2,16,256]{4,3,2,1,0:T(8,128)}, u32[]{:S(2)}) copy-start(f32[1,5,2,16,256]{4,3,2,1,0:T(8,128)} %param.8) | copy-start | bytes 491524
  44.5 1.7 %copy-start.1 = (f32[160,256]{1,0:T(8,128)S(1)}, f32[160,256]{1,0:T(8,128)}, u32[]{:S(2)}) copy-start(f32[160,256]{1,0:T(8,128)} %get-tuple-element.4) | copy-start | bytes 491524

commit v5 on v4

--- a/solution.py
+++ b/solution.py
@@ -151,8 +151,8 @@
 
 def kernel(
     old_hbm, init_hbm, force_hbm, owner_hbm, forward_hbm, inverse_hbm, back_hbm, table_hbm,
-    ends_hbm, before_hbm,
-    init_ref, owner_ref, forward_ref, inverse_ref, back_ref, table, stacked, out1, in1, state, first, out2, in2, out3, in3, out6, in6, packed, gathered, fine, ends,
+    ends, before_hbm,
+    init_ref, owner_ref, forward_ref, inverse_ref, back_ref, table, stacked, out1, in1, state, first, out2, in2, out3, in3, out6, in6, packed, gathered, fine,
     load, send1, recv1, send2, recv2, send3, recv3, send4, recv4, send5, recv5, send6, recv6, store,
 ):
     n = lax.axis_index("cuts")
@@ -184,11 +184,11 @@
         return c
 
     def greet_cuts(k, c):
-        pl.semaphore_signal(barrier, inc=1, device_id={"cuts": lax.rem(n + k, CUTS)}, device_id_type=MESH)
+        pl.semaphore_signal(barrier, inc=1, device_id={"cuts": n - k}, device_id_type=MESH)
         return c
 
     lax.fori_loop(1, SPACE, greet_space, 0, unroll=True)
-    lax.fori_loop(1, CUTS, greet_cuts, 0, unroll=True)
+    lax.fori_loop(1, n + 1, greet_cuts, 0)
 
     for copy in loads:
         copy.start()
@@ -221,7 +221,7 @@
             else:
                 out6[:, at // 2 - 2 * NVAR, at % 2, :] = by_row[r]
 
-    pl.semaphore_wait(barrier, SPACE + CUTS - 2)
+    pl.semaphore_wait(barrier, SPACE - 1 + CUTS - 1 - n)
 
     def exchange(source, target, send, recv):
         def start(k, c):
@@ -373,7 +373,7 @@
         )
 
     def keep_initial():
-        return pltpu.make_async_copy(init_ref, before_hbm, store.at[1])
+        return pltpu.make_async_copy(init_ref, before_hbm, store)
 
     @pl.when(n < CUTS - 1)
     def _():
@@ -395,9 +395,6 @@
         for i in range(2):
             at = slice((2 * v + i) * NY, (2 * v + i + 1) * NY)
             ends[at] = fine[at] + change[v * NY : (v + 1) * NY]
-    keep_ends = pltpu.make_async_copy(ends, ends_hbm, store.at[0])
-    keep_ends.start()
-
     def sent_gain(k, c):
         send_gain(k).wait_send()
         return c
@@ -415,8 +412,6 @@
     @pl.when(n == 0)
     def _():
         keep_initial().wait()
-
-    keep_ends.wait()
 
 
 def body(old_starts, initial, blade_force, blade_owner):
@@ -427,7 +422,7 @@
         kernel,
         out_shape=[jax.ShapeDtypeStruct((rows, NZ), f32) for rows in (ROWS, ROWS)],
         in_specs=[hbm] * 8,
-        out_specs=[hbm] * 2,
+        out_specs=[pl.BlockSpec(memory_space=pltpu.VMEM), hbm],
         scratch_shapes=[
             pltpu.VMEM((ROWS, NZ), f32),
             pltpu.SMEM((STEPS, CUTS), jnp.int32),
@@ -449,7 +444,6 @@
             pltpu.VMEM((8 * NVAR, LANES), f32),
             pltpu.VMEM((CUTS, 8 * NVAR, LANES), f32),
             pltpu.VMEM((ROWS, NZ), f32),
-            pltpu.VMEM((ROWS, NZ), f32),
             dma((8,)),
             dma,
             dma,
@@ -463,10 +457,10 @@
             dma,
             dma,
             dma,
-            dma((2,)),
+            dma,
         ],
         compiler_params=pltpu.CompilerParams(
-            collective_id=0, has_side_effects=True, vmem_limit_bytes=56 * 2**20
+            collective_id=0, has_side_effects=True, vmem_limit_bytes=54800 * 1024
         ),
     )(
         old_starts.reshape(ROWS, NZ),

time: 47 us -> 46.6 us (level)
  other arithmetic: 1.64 us -> 0.69 us
  local copies, waits for them, and re-layouts: 0.67 us -> 1.34 us
    sub x1, other arithmetic: 1.64 us -> 0.69 us  [body(): return (ends.reshape(shape), old_starts - before.reshape(shape))]
    unnamed x5, local copies, waits for them, and re-layouts: 0.67 us -> 1.34 us
where the time goes in v5:
time: 46.6 us; the launch traced here: 46.4 us
  Pallas kernels  43.7 us (94%)
  local copies, waits for them, and re-layouts  1.34 us (3%)
  other arithmetic  0.69 us (1%)
  between operations  0.66 us (1%)
    pallas_call x1, Pallas kernels, body(): pl.pallas_call(kernel, out_shape=[jax.ShapeDtypeStruct((rows, NZ), f32) f...  43.7 us
    unnamed x5, local copies, waits for them, and re-layouts  1.34 us

profile of v5, /device:TPU:2, one launch (start us, length us, event | category | flops | bytes accessed | tf_op | source)
XLA Modules:
  0.0 46.4 jit_solution(16081743070106986530)
XLA Ops:
  0.6 0.0 copy-start
  0.6 0.7 %copy-done = s32[16,3]{0,1:T(4,128)S(1)} copy-done((s32[16,3]{0,1:T(4,128)S(1)}, s32[16,3]{0,1:T(4,128)}, u32[]{:S(2)}) %copy-start) | copy-done | bytes 216
  1.3 0.0 copy-start.1
  1.3 43.7 %shard_map.95 = (f32[160,256]{1,0:T(8,128)S(1)}, f32[160,256]{1,0:T(8,128)S(1)}) custom-call(f32[160,256]{1,0:T(8,128)} %bitcast.9, f32[160,256]{1,0:T(8,128)} %bitcast.10, f32[160,256]{1,0:T(8,128)} %bitcast.11, s32[3,16]{1,0:T(4,128)S(1)} %bitcast.8, bf16[256,768]{1,0:T(8,128)(2,1)} %constant.8.clone.forward_hbm, ...), custom_call_target="tpu_custom_call" | custom-call | tf_op jit(solution)/shard_map/pallas_call | solution.py:421
  45.1 0.0 copy-done.1
  45.1 0.7 %sub.3 = f32[1,5,2,16,256]{4,3,2,1,0:T(8,128)} subtract(f32[1,5,2,16,256]{4,3,2,1,0:T(8,128)S(1)} %copy-done.1, f32[1,5,2,16,256]{4,3,2,1,0:T(8,128)S(1)} %bitcast.7) | non-fusion elementwise | flops 40960 | bytes 491520 | tf_op jit(solution)/shard_map/sub | solution.py:476
  45.8 0.7 %copy.11 = f32[1,5,2,16,256]{4,3,2,1,0:T(8,128)} copy(f32[1,5,2,16,256]{4,3,2,1,0:T(8,128)S(1)} %bitcast.6) | data formatting | bytes 327680
Async XLA Ops:
  0.6 0.7 %copy-start = (s32[16,3]{0,1:T(4,128)S(1)}, s32[16,3]{0,1:T(4,128)}, u32[]{:S(2)}) copy-start(s32[16,3]{0,1:T(4,128)} %param.11) | copy-start | bytes 580
  1.3 43.8 %copy-start.1 = (f32[1,5,2,16,256]{4,3,2,1,0:T(8,128)S(1)}, f32[1,5,2,16,256]{4,3,2,1,0:T(8,128)}, u32[]{:S(2)}) copy-start(f32[1,5,2,16,256]{4,3,2,1,0:T(8,128)} %param.8) | copy-start | bytes 491524

commit v6 on v5

--- a/solution.py
+++ b/solution.py
@@ -246,7 +246,6 @@
     begin1, finish1 = exchange(out1, in1, send1, recv1)
     begin6, finish6 = exchange(out6, in6, send6, recv6)
     begin1()
-    begin6()
     for copy in loads[4:]:
         copy.wait()
     finish1()
@@ -322,6 +321,8 @@
         @pl.when(n + k < CUTS)
         def _():
             send_gain(k).start()
+
+    begin6()
 
     for v in range(NVAR):
         for i in range(2):

time: 46.6 us -> 47.5 us (1.019)
  Pallas kernels: 43.7 us -> 44.6 us
    pallas_call x1, Pallas kernels: 43.7 us -> 44.6 us  [body(): pl.pallas_call(kernel, out_shape=[jax.ShapeDtypeStruct((rows, NZ), f32) f...]
where the time goes in v6:
time: 47.5 us; the launch traced here: 47.3 us
  Pallas kernels  44.6 us (94%)
  local copies, waits for them, and re-layouts  1.34 us (3%)
  other arithmetic  0.69 us (1%)
  between operations  0.66 us (1%)
    pallas_call x1, Pallas kernels, body(): pl.pallas_call(kernel, out_shape=[jax.ShapeDtypeStruct((rows, NZ), f32) f...  44.6 us
    unnamed x5, local copies, waits for them, and re-layouts  1.34 us

profile of v6, /device:TPU:2, one launch (start us, length us, event | category | flops | bytes accessed | tf_op | source)
XLA Modules:
  0.0 47.3 jit_solution(14788095756538271316)
XLA Ops:
  0.6 0.0 copy-start
  0.6 0.7 %copy-done = s32[16,3]{0,1:T(4,128)S(1)} copy-done((s32[16,3]{0,1:T(4,128)S(1)}, s32[16,3]{0,1:T(4,128)}, u32[]{:S(2)}) %copy-start) | copy-done | bytes 216
  1.3 0.0 copy-start.1
  1.3 44.6 %shard_map.95 = (f32[160,256]{1,0:T(8,128)S(1)}, f32[160,256]{1,0:T(8,128)S(1)}) custom-call(f32[160,256]{1,0:T(8,128)} %bitcast.9, f32[160,256]{1,0:T(8,128)} %bitcast.10, f32[160,256]{1,0:T(8,128)} %bitcast.11, s32[3,16]{1,0:T(4,128)S(1)} %bitcast.8, bf16[256,768]{1,0:T(8,128)(2,1)} %constant.8.clone.forward_hbm, ...), custom_call_target="tpu_custom_call" | custom-call | tf_op jit(solution)/shard_map/pallas_call | solution.py:422
  46.0 0.0 copy-done.1
  46.0 0.7 %sub.3 = f32[1,5,2,16,256]{4,3,2,1,0:T(8,128)} subtract(f32[1,5,2,16,256]{4,3,2,1,0:T(8,128)S(1)} %copy-done.1, f32[1,5,2,16,256]{4,3,2,1,0:T(8,128)S(1)} %bitcast.7) | non-fusion elementwise | flops 40960 | bytes 491520 | tf_op jit(solution)/shard_map/sub | solution.py:477
  46.7 0.7 %copy.11 = f32[1,5,2,16,256]{4,3,2,1,0:T(8,128)} copy(f32[1,5,2,16,256]{4,3,2,1,0:T(8,128)S(1)} %bitcast.6) | data formatting | bytes 327680
Async XLA Ops:
  0.6 0.7 %copy-start = (s32[16,3]{0,1:T(4,128)S(1)}, s32[16,3]{0,1:T(4,128)}, u32[]{:S(2)}) copy-start(s32[16,3]{0,1:T(4,128)} %param.11) | copy-start | bytes 580
  1.3 44.7 %copy-start.1 = (f32[1,5,2,16,256]{4,3,2,1,0:T(8,128)S(1)}, f32[1,5,2,16,256]{4,3,2,1,0:T(8,128)}, u32[]{:S(2)}) copy-start(f32[1,5,2,16,256]{4,3,2,1,0:T(8,128)} %param.8) | copy-start | bytes 491524
